TPU v7x, 32 devices: a whole 2x2x4 slice. The times are simulated.
32 devices in a mesh: alpha: 8 (over z, core), beta: 4 (over y, x).
Axes of the slice: x: 2, y: 2, z: 4, core: 2. Of those that a mesh axis runs over, the one named last changes fastest.
Arguments:
- ci_vector: float32 [1024, 24576], P('alpha', 'beta'), may hold values from -6 to 6
- patterns: float32 [16, 64, 64], replicated, may hold values from -0.7 to 2
- alpha_links: int32 [16, 8], replicated, may hold values from 0 to 15
- alpha_kinds: int32 [16, 8], replicated, may hold values from 0 to 15
- alpha_coefs: float32 [16, 8], replicated, may hold values from -1 to 1
- beta_links: int32 [384, 2], replicated, may hold values from 0 to 383
- beta_kinds: int32 [384, 2], replicated, may hold values from 0 to 15
- beta_coefs: float32 [384, 2], replicated, may hold values from -1 to 1
Outputs:
- sigma: float32 [1024, 24576], P('alpha', 'beta')
All inputs are finite; a program needn't handle non-finite values.
Results may differ from a plain program's by a relative error of at most 0.0001.
Values sent between devices are 32-bit elements; how exact they have to be, the bound alone decides.
No kernel may reach another device: no remote copies, remote signals or barrier semaphores. Data moves between devices by JAX's collectives and lax.ppermute only.
A program may use at most 192 MiB of HBM per device.

v0:
```python
import jax
import jax.numpy as jnp
from jax import lax
from jax.sharding import PartitionSpec as P

BLK = 64


def beta_term(row_data, patterns, links, kinds, coefs):
    block_count = links.shape[0]
    slot_count = links.shape[1]
    strided = row_data.reshape(row_data.shape[0], block_count, BLK)
    matrices = patterns[kinds] * coefs[:, :, None, None]
    gathered = strided[:, links.reshape(-1), :].reshape(
        row_data.shape[0], block_count, slot_count, BLK
    )
    result = jnp.einsum("ajsq,jsqp->ajp", gathered, matrices, precision=lax.Precision.HIGHEST)
    return result.reshape(row_data.shape)


def on_device(
    ci_vector, patterns, alpha_links, alpha_kinds, alpha_coefs, beta_links, beta_kinds, beta_coefs
):
    regrouped = lax.all_to_all(ci_vector, "beta", split_axis=0, concat_axis=1, tiled=True)
    beta_rows = beta_term(regrouped, patterns, beta_links, beta_kinds, beta_coefs)
    beta_part = lax.all_to_all(beta_rows, "beta", split_axis=1, concat_axis=0, tiled=True)
    own_count = ci_vector.shape[0] // BLK
    own_block = lax.axis_index("alpha") * own_count
    own_links = lax.dynamic_slice_in_dim(alpha_links, own_block, own_count, 0)
    own_kinds = lax.dynamic_slice_in_dim(alpha_kinds, own_block, own_count, 0)
    own_coefs = lax.dynamic_slice_in_dim(alpha_coefs, own_block, own_count, 0)
    own_matrices = patterns[own_kinds] * own_coefs[:, :, None, None]
    piece = lax.all_gather(ci_vector, "alpha", axis=0, tiled=True)
    piece_blocks = piece.shape[0] // BLK
    targets = jnp.arange(piece_blocks, dtype=jnp.int32)
    matches = (own_links[:, :, None] == targets[None, None, :]).astype(jnp.float32)
    coupling = jnp.einsum("osk,ospq->opkq", matches, own_matrices, precision=lax.Precision.HIGHEST)
    coupling = coupling.reshape(own_count * BLK, piece_blocks * BLK)
    alpha_part = jnp.dot(
        coupling, piece, precision=lax.Precision.HIGHEST, preferred_element_type=jnp.float32
    )
    return alpha_part + beta_part


def solution(mesh):
    return jax.shard_map(
        on_device,
        mesh=mesh,
        in_specs=(P("alpha", "beta"), P(), P(), P(), P(), P(), P(), P()),
        out_specs=P("alpha", "beta"),
        check_vma=False,
    )
```

profile of v0, /device:TPU:0, one launch (start us, length us, event | category | flops | bytes accessed | tf_op | source)
XLA Modules:
  0.0 258.4 jit_solution(13709491477177525988)
XLA Ops:
  6.5 0.0 copy-start
  6.5 0.0 all-gather.2.cloned.1.call-start
  6.5 0.7 all-gather.2.cloned.1.call-update
  7.3 5.2 %all-to-all-start = ((f32[4,32,6144]{2,1,0:T(8,128)}), f32[4,32,6144]{2,1,0:T(8,128)}, u32[]{:S(2)}, u32[]{:S(2)}) async-start(f32[4,32,6144]{2,1,0:T(8,128)} %bitcast.29), calls=%async_computation | async-start | bytes 6291456 | tf_op jit(solution)/shard_map/all_to_all | solution.py:24
  12.4 0.8 copy.32
  13.3 0.2 reshape.54
  13.4 0.7 compare_select_fusion.1
  14.1 0.1 copy.29
  14.3 0.1 reshape.66
  14.4 0.8 copy.30
  15.2 0.0 copy-done
  15.3 13.3 %gather_fusion.1 = f32[768,64,64]{2,1,0:T(8,128)} fusion(f32[16,64,64]{2,1,0:T(8,128)S(1)} %copy-done, s32[1024]{0:T(1024)S(1)} %pad_clamp_fusion.1), kind=kCustom, calls=%fused_computation.1 | custom fusion | bytes 25168896 | tf_op jit(solution)/shard_map/gather | solution.py:13
  28.6 21.0 %all-to-all-done = f32[4,32,6144]{2,1,0:T(8,128)} async-done(((f32[4,32,6144]{2,1,0:T(8,128)}), f32[4,32,6144]{2,1,0:T(8,128)}, u32[]{:S(2)}, u32[]{:S(2)}) %all-to-all-start) | async-done | bytes 3145760 | tf_op jit(solution)/shard_map/all_to_all | solution.py:24
  49.6 5.6 %copy.31 = f32[32,4,6144]{2,1,0:T(4,128)} copy(f32[32,4,6144]{2,0,1:T(8,128)} %bitcast.6) | data formatting | bytes 6291456 | tf_op jit(solution)/shard_map/all_to_all | solution.py:24
  55.2 6.6 %reshape.53 = f32[32,384,64]{2,1,0:T(8,128)} reshape(f32[32,4,6144]{2,1,0:T(4,128)} %copy.31) | data formatting | bytes 6291456 | tf_op jit(solution)/shard_map/reshape | solution.py:12
  61.7 9.1 %copy.33 = f32[32,384,64]{2,0,1:T(8,128)} copy(f32[32,384,64]{2,1,0:T(8,128)} %reshape.53) | data formatting | bytes 6291456 | tf_op jit(solution)/shard_map/reshape | solution.py:12
  70.9 10.1 %gather_fusion.2 = f32[768,32,64]{2,1,0:T(8,128)} fusion(f32[32,384,64]{2,0,1:T(8,128)} %copy.33, s32[1024]{0:T(1024)S(1)} %pad_clamp_fusion), kind=kCustom, calls=%fused_computation.2 | custom fusion | bytes 12585984 | tf_op jit(solution)/shard_map/gather | solution.py:14
  81.0 27.4 %fusion.3 = f32[32,384,64]{2,0,1:T(8,128)S(1)} fusion(f32[32,384,2,64]{3,0,2,1:T(8,128)} %bitcast.28, f32[384,2,64,64]{3,2,1,0:T(8,128)} %bitcast.27, f32[384,2]{1,0:T(8,128)S(1)} %copy.30), kind=kOutput, calls=%fused_computation.7 | convolution fusion | flops 1211105280 | bytes 22023168 | tf_op jit(solution)/shard_map/ajsq,jsqp->ajp/dot_general | solution.py:17
  108.4 6.3 %copy.34 = f32[32,384,64]{2,1,0:T(8,128)} copy(f32[32,384,64]{2,0,1:T(8,128)S(1)} %fusion.3) | data formatting | bytes 6291456 | tf_op jit(solution)/shard_map/ajsq,jsqp->ajp/transpose | solution.py:17
  114.8 0.0 copy-start.2
  114.8 0.0 copy-start.3
  114.8 0.0 copy-start.1
  114.8 6.8 %all_to_all.29 = f32[32,4,6144]{2,1,0:T(4,128)} reshape(f32[32,384,64]{2,1,0:T(8,128)} %copy.34) | data formatting | bytes 6291456 | tf_op jit(solution)/shard_map/all_to_all | solution.py:26
  121.6 5.5 %copy.35 = f32[32,4,6144]{2,0,1:T(8,128)} copy(f32[32,4,6144]{2,1,0:T(4,128)} %all_to_all.29) | data formatting | bytes 6291456 | tf_op jit(solution)/shard_map/all_to_all | solution.py:26
  127.0 4.8 %all-to-all-start.1 = ((f32[32,4,6144]{2,0,1:T(8,128)}), f32[32,4,6144]{2,0,1:T(8,128)}, u32[]{:S(2)}, u32[]{:S(2)}) async-start(f32[32,4,6144]{2,0,1:T(8,128)} %copy.35), calls=%async_computation.1 | async-start | bytes 6291456 | tf_op jit(solution)/shard_map/all_to_all | solution.py:26
  131.8 0.0 copy-done.2
  131.8 0.0 copy-done.3
  131.9 0.1 compare_select_fusion.2
  131.9 0.1 copy.25
  132.0 0.1 reshape.58
  132.1 0.6 gather_fusion
  132.7 0.0 copy-done.1
  132.7 0.1 constant_dynamic-slice_fusion.1
  132.8 0.1 copy.26
  132.9 0.1 copy.28
  133.0 0.9 convolution_bitcast_fusion
  133.8 0.3 reshape.52
  134.1 33.6 %all-to-all-done.1 = f32[32,4,6144]{2,0,1:T(8,128)} async-done(((f32[32,4,6144]{2,0,1:T(8,128)}), f32[32,4,6144]{2,0,1:T(8,128)}, u32[]{:S(2)}, u32[]{:S(2)}) %all-to-all-start.1) | async-done | bytes 3145760 | tf_op jit(solution)/shard_map/all_to_all | solution.py:26
  167.7 63.9 %all-gather.2.cloned.1.call-done = f32[1024,6144]{1,0:T(8,128)} async-done(((f32[128,6144]{1,0:T(8,128)}), f32[1024,6144]{1,0:T(8,128)}) %all-gather.2.cloned.1.call-update) | async-done | bytes 25165840 | tf_op jit(solution)/shard_map/all_gather | solution.py:33
  231.6 19.9 %convolution_add_fusion = f32[128,6144]{1,0:T(8,128)} fusion(f32[128,6144]{1,0:T(8,128)} %bitcast.13, f32[128,1024]{1,0:T(8,128)S(1)} %reshape.52, f32[1024,6144]{1,0:T(8,128)} %all-gather.2.cloned.1.call-done), kind=kOutput, calls=%fused_computation.6 | convolution fusion | flops 9664462848 | bytes 31981568 | tf_op jit(solution)/shard_map/dot_general | solution.py:39
  (4 shorter events, 0.0 us)
Async XLA Ops:
  6.5 8.7 %copy-start = (f32[16,64,64]{2,1,0:T(8,128)S(1)}, f32[16,64,64]{2,1,0:T(8,128)}, u32[]{:S(2)}) copy-start(f32[16,64,64]{2,1,0:T(8,128)} %param.9) | copy-start | bytes 786436
  6.5 225.1 %all-gather.2.cloned.1.call-start = ((), (), s32[]{:S(2)}) async-start(), calls=%async_computation.2 | async-start | bytes 28311552 | tf_op jit(solution)/shard_map/all_gather | solution.py:33
  7.3 42.3 %all-to-all-start = ((f32[4,32,6144]{2,1,0:T(8,128)}), f32[4,32,6144]{2,1,0:T(8,128)}, u32[]{:S(2)}, u32[]{:S(2)}) async-start(f32[4,32,6144]{2,1,0:T(8,128)} %bitcast.29), calls=%async_computation | async-start | bytes 6291456 | tf_op jit(solution)/shard_map/all_to_all | solution.py:24
  114.8 17.1 %copy-start.2 = (s32[16,8]{0,1:T(8,128)S(1)}, s32[16,8]{0,1:T(8,128)}, u32[]{:S(2)}) copy-start(s32[16,8]{0,1:T(8,128)} %param.11) | copy-start | bytes 1540
  114.8 17.1 %copy-start.3 = (s32[16,8]{0,1:T(8,128)S(1)}, s32[16,8]{0,1:T(8,128)}, u32[]{:S(2)}) copy-start(s32[16,8]{0,1:T(8,128)} %param.10) | copy-start | bytes 1540
  114.8 17.9 %copy-start.1 = (f32[16,8]{0,1:T(8,128)S(1)}, f32[16,8]{0,1:T(8,128)}, u32[]{:S(2)}) copy-start(f32[16,8]{0,1:T(8,128)} %param.12) | copy-start | bytes 1540
  127.0 40.7 %all-to-all-start.1 = ((f32[32,4,6144]{2,0,1:T(8,128)}), f32[32,4,6144]{2,0,1:T(8,128)}, u32[]{:S(2)}, u32[]{:S(2)}) async-start(f32[32,4,6144]{2,0,1:T(8,128)} %copy.35), calls=%async_computation.1 | async-start | bytes 6291456 | tf_op jit(solution)/shard_map/all_to_all | solution.py:26
Sparse Core Ops, SparseCore 0:
  9.0 222.5 all-gather.1
where the time goes:
time: 259 us; the launch traced here: 258 us
  waiting for transfers between devices  119 us (46%)
  local copies, waits for them, and re-layouts  66.7 us (26%)
  matrix products  48.2 us (19%)
  between operations  13.5 us (5%)
  starting transfers between devices  9.97 us (4%)
    all_gather x1, waiting for transfers between devices, on_device(): piece = lax.all_gather(ci_vector, 'alpha', axis=0, tiled=True)  63.9 us
    all_to_all x1, waiting for transfers between devices, on_device(): lax.all_to_all(beta_rows, 'beta', split_axis=1, concat_axis=0, tiled=True)  33.6 us
    dot_general x1, matrix products, beta_term(): jnp.einsum('ajsq,jsqp->ajp', gathered, matrices, precision=lax.Precision....  27.4 us
    all_to_all x1, waiting for transfers between devices, on_device(): lax.all_to_all(ci_vector, 'beta', split_axis=0, concat_axis=1, tiled=True)  21 us
    dot_general x1, matrix products, on_device(): jnp.dot(coupling, piece, precision=lax.Precision.HIGHEST, preferred_eleme...  19.9 us
    reshape x2, local copies, waits for them, and re-layouts, beta_term(): strided = row_data.reshape(row_data.shape[0], block_count, BLK)  15.7 us
    gather x1, local copies, waits for them, and re-layouts, beta_term(): matrices = patterns[kinds] * coefs[:, :, None, None]  13.3 us
    all_to_all x2, local copies, waits for them, and re-layouts, on_device(): lax.all_to_all(beta_rows, 'beta', split_axis=1, concat_axis=0, tiled=True)  12.3 us
  transfers between devices with their start and end apart: 3, of which 3 were waited for; matrix products, arithmetic and copies ran while one was open for 34% of the time, Pallas kernels for 0%

commit v1 on v0

v1 whole, which is shorter than its diff:
```python
import functools

import jax
import jax.numpy as jnp
from jax import lax
from jax.experimental import pallas as pl
from jax.experimental.pallas import tpu as pltpu
from jax.sharding import PartitionSpec as P

BLK = 64
LANES = 128
CHUNKS = 2


def split(value):
    high = value.astype(jnp.bfloat16)
    low = (value - high.astype(jnp.float32)).astype(jnp.bfloat16)
    return high, low


def dot3(left, right):
    dot = functools.partial(jnp.dot, preferred_element_type=jnp.float32)
    return dot(left[0], right[0]) + (dot(left[0], right[1]) + dot(left[1], right[0]))


def alpha_kernel(count, matrix_ref, *refs):
    piece_refs = refs[:count]
    own_ref, send_ref, matrix_high, matrix_low, piece_high, piece_low = refs[count:]

    @pl.when(pl.program_id(0) == 0)
    def _():
        matrix_high[...], matrix_low[...] = split(matrix_ref[...])

    rows = own_ref.shape[0]
    for index, piece_ref in enumerate(piece_refs):
        place = pl.ds(index * rows, rows)
        piece_high[place, :], piece_low[place, :] = split(piece_ref[...])
    product = dot3(
        (matrix_high[...], matrix_low[...]), (piece_high[...], piece_low[...])
    )
    own_ref[...] = product[:rows]
    send_ref[...] = product[rows:]


def alpha_products(matrix, whole, pieces, start, width):
    rows = whole[0].shape[0]
    tile = width
    while tile > 768:
        tile //= 2
    count = len(whole) + len(pieces)
    depth = count * rows
    first = start // tile
    out = jax.ShapeDtypeStruct((rows, width), jnp.float32)
    return pl.pallas_call(
        functools.partial(alpha_kernel, count),
        grid=(width // tile,),
        in_specs=[pl.BlockSpec((2 * rows, depth), lambda i: (0, 0))]
        + [pl.BlockSpec((rows, tile), lambda i: (0, first + i))] * len(whole)
        + [pl.BlockSpec((rows, tile), lambda i: (0, i))] * len(pieces),
        out_specs=[pl.BlockSpec((rows, tile), lambda i: (0, i))] * 2,
        out_shape=[out, out],
        scratch_shapes=[pltpu.VMEM((2 * rows, depth), jnp.bfloat16)] * 2
        + [pltpu.VMEM((depth, tile), jnp.bfloat16)] * 2,
        compiler_params=pltpu.CompilerParams(vmem_limit_bytes=40 * 2**20),
        cost_estimate=pl.CostEstimate(
            flops=12 * rows * depth * width,
            bytes_accessed=4 * (depth + 2 * rows) * width,
            transcendentals=0,
        ),
    )(matrix, *whole, *pieces)


def coupling_matrix(patterns, links, kinds, coefs, target_blocks, source_blocks):
    links, kinds, coefs = links[target_blocks], kinds[target_blocks], coefs[target_blocks]
    matrices = patterns[kinds] * coefs[:, :, None, None]
    matches = (links[:, :, None] == source_blocks).astype(jnp.float32)
    coupling = jnp.einsum("osk,ospq->opkq", matches, matrices, precision=lax.Precision.HIGHEST)
    return coupling.reshape(target_blocks.shape[0] * BLK, source_blocks.shape[0] * BLK)


def beta_kernel(
    layout, me_ref, slot_ref, tile_ref, half_ref, kind_ref, coef_ref, pattern_ref, *refs
):
    parts = refs[: len(layout)]
    out_ref, data, pattern_high, pattern_low, sems = refs[len(layout) :]
    copies = []
    for index, ((flip, row, count), part) in enumerate(zip(layout, parts)):
        slot = lax.bitwise_xor(me_ref[0], flip)
        copies.append(
            pltpu.make_async_copy(part, data.at[slot, pl.ds(row, count)], sems.at[index])
        )
    for copy in copies:
        copy.start()
    pattern_high[...], pattern_low[...] = split(pattern_ref[...])
    for copy in copies:
        copy.wait()
    rows = out_ref.shape[0]
    lower = lax.broadcasted_iota(jnp.int32, (rows, LANES), 1) < BLK

    def block(item, side):
        lanes = pl.ds(pl.multiple_of(tile_ref[item] * LANES, LANES), LANES)
        value = data[slot_ref[item], :, lanes] * coef_ref[item]
        return pltpu.roll(value, BLK * lax.bitwise_xor(half_ref[item], side), 1)

    def pair(index, carry):
        first = index * 4
        left, right = [], []
        for side in (0, 1):
            item = first + 2 * side
            left.append(split(jnp.where(lower, block(item, 0), block(item + 1, 1))))
            for slot in (0, 1):
                kind = kind_ref[item + slot] * 2 + side
                right.append((pattern_high[kind], pattern_low[kind]))
        left = [jnp.concatenate([part[half] for part in left], 1) for half in (0, 1)]
        right = [jnp.concatenate([part[half] for part in right], 0) for half in (0, 1)]
        out_ref[:, pl.ds(pl.multiple_of(index * LANES, LANES), LANES)] = dot3(left, right)
        return carry

    lax.fori_loop(0, out_ref.shape[1] // LANES, pair, 0, unroll=2)


def beta_term(me, device_count, layout, parts, patterns, links, kinds, coefs, shape):
    rows, cols = shape
    own_count = cols // BLK
    own = [
        lax.dynamic_slice_in_dim(array, me * own_count, own_count, 0).reshape(-1)
        for array in (links, kinds, coefs)
    ]
    owner, place = own[0] // own_count, own[0] % own_count
    zeros = jnp.zeros_like(patterns)
    sides = jnp.stack(
        [jnp.concatenate([patterns, zeros], 2), jnp.concatenate([zeros, patterns], 2)], 1
    ).reshape(-1, BLK, LANES)
    smem = pl.BlockSpec(memory_space=pltpu.SMEM)
    vmem = pl.BlockSpec(memory_space=pltpu.VMEM)
    return pl.pallas_call(
        functools.partial(beta_kernel, layout),
        in_specs=[smem] * 6 + [vmem] + [pl.BlockSpec(memory_space=pl.ANY)] * len(parts),
        out_specs=vmem,
        out_shape=jax.ShapeDtypeStruct(shape, jnp.float32),
        scratch_shapes=[
            pltpu.VMEM((device_count, rows, cols), jnp.float32),
            pltpu.VMEM(sides.shape, jnp.bfloat16),
            pltpu.VMEM(sides.shape, jnp.bfloat16),
            pltpu.SemaphoreType.DMA((len(parts),)),
        ],
        compiler_params=pltpu.CompilerParams(vmem_limit_bytes=40 * 2**20),
        cost_estimate=pl.CostEstimate(
            flops=12 * rows * cols * 4 * BLK,
            bytes_accessed=4 * rows * cols * (device_count + 1),
            transcendentals=0,
        ),
    )(me.reshape(1), owner, place // 2, place % 2, own[1], own[2], sides, *parts)


def on_device(
    alpha_devices,
    beta_devices,
    ci_vector,
    patterns,
    alpha_links,
    alpha_kinds,
    alpha_coefs,
    beta_links,
    beta_kinds,
    beta_coefs,
):
    rows, cols = ci_vector.shape
    layers = alpha_devices // 2
    width = cols // (2 * CHUNKS)
    me = lax.axis_index("alpha")
    me_beta = lax.axis_index("beta")

    def over_alpha(value, flip):
        return lax.ppermute(value, "alpha", [(i, i ^ flip) for i in range(alpha_devices)])

    def over_beta(value, flip):
        return lax.ppermute(value, "beta", [(i, i ^ flip) for i in range(beta_devices)])

    plans = [
        ([2 * m for m in range(1, layers // 2)], layers),
        ([4 * m for m in range(1, layers // 2)], 2),
    ]
    peer = over_alpha(ci_vector, 1)
    arrived = {}
    for chunk in range(CHUNKS):
        for kind, (members, _) in enumerate(plans):
            start = (kind * CHUNKS + chunk) * width
            piece = ci_vector[:, start : start + width]
            arrived[kind, chunk] = [over_alpha(piece, flip) for flip in members]

    gathered = {0: ci_vector}
    layout, parts = [(0, 0, rows)], [ci_vector]
    for flip in range(1, beta_devices):
        low = flip & -flip
        if low == flip:
            gathered[flip] = over_beta(ci_vector, flip)
            layout.append((flip, 0, rows))
            parts.append(gathered[flip])
    for flip in range(1, beta_devices):
        low = flip & -flip
        if low != flip:
            top = over_beta(gathered[flip ^ low][: rows // 2], low)
            bottom = over_beta(gathered[low][rows // 2 :], flip ^ low)
            gathered[flip] = jnp.concatenate([top, bottom], 0)
            layout += [(flip, 0, rows // 2), (flip, rows // 2, rows // 2)]
            parts += [top, bottom]

    blocks = rows // BLK
    inner = jnp.arange(blocks, dtype=jnp.int32)
    sums = {}
    for kind, (members, partner) in enumerate(plans):
        sources = [0, 1] + [flip ^ core for flip in members for core in (0, 1)]
        targets = jnp.concatenate([(me ^ flip) * blocks + inner for flip in (0, partner)])
        source_blocks = jnp.concatenate([(me ^ flip) * blocks + inner for flip in sources])
        matrix = coupling_matrix(
            patterns, alpha_links, alpha_kinds, alpha_coefs, targets, source_blocks
        )
        for chunk in range(CHUNKS):
            pieces = []
            for piece in arrived[kind, chunk]:
                pieces += [piece, over_alpha(piece, 1)]
            start = (kind * CHUNKS + chunk) * width
            own, send = alpha_products(matrix, [ci_vector, peer], pieces, start, width)
            sums[kind, chunk] = own, over_alpha(send, partner)

    beta_part = beta_term(
        me_beta,
        beta_devices,
        tuple(layout),
        parts,
        patterns,
        beta_links,
        beta_kinds,
        beta_coefs,
        (rows, cols),
    )
    order = [sums[kind, chunk] for kind in (0, 1) for chunk in range(CHUNKS)]
    own = jnp.concatenate([own for own, _ in order], 1)
    other = jnp.concatenate([other for _, other in order], 1)
    return (own + beta_part) + other


def solution(mesh):
    return jax.shard_map(
        functools.partial(on_device, mesh.shape["alpha"], mesh.shape["beta"]),
        mesh=mesh,
        in_specs=(P("alpha", "beta"), P(), P(), P(), P(), P(), P(), P()),
        out_specs=P("alpha", "beta"),
        check_vma=False,
    )
```

time: 259 us -> 208 us (0.80)
  matrix products: 48.2 us -> 6.72 us
  local copies, waits for them, and re-layouts: 66.7 us -> 33.9 us
  Pallas kernels: 0 us -> 28.5 us
  between operations: 13.5 us -> 0.19 us
  starting transfers between devices: 9.97 us -> 15.2 us
  other arithmetic: 0.81 us -> 4.57 us
    ppermute x0 -> x17, waiting for transfers between devices: none -> 118 us  [the longest x13 108 us: over_alpha(): lax.ppermute(value, 'alpha', [(i, i ^ flip) for i in range(alpha_devices)])]
    all_gather x1 -> x0, waiting for transfers between devices: 63.9 us -> none  [on_device(): piece = lax.all_gather(ci_vector, 'alpha', axis=0, tiled=True)]
    all_to_all x2 -> x0, waiting for transfers between devices: 54.6 us -> none  [the longest x1 33.6 us: on_device(): lax.all_to_all(beta_rows, 'beta', split_axis=1, concat_axis=0, tiled=True)]
    dot_general x3 -> x2, matrix products: 48.2 us -> 6.72 us  [coupling_matrix(): jnp.einsum('osk,ospq->opkq', matches, matrices, precision=lax.Precision.H...]
    pallas_call x0 -> x5, Pallas kernels: none -> 28.5 us  [the longest x4 14.8 us: alpha_products(): pl.pallas_call(functools.partial(alpha_kernel, count), grid=(width // til...]
    all_to_all x3 -> x0, local copies, waits for them, and re-layouts: 17.8 us -> none  [the longest x2 12.3 us: on_device(): lax.all_to_all(beta_rows, 'beta', split_axis=1, concat_axis=0, tiled=True)]
    ppermute x0 -> x17, starting transfers between devices: none -> 15.2 us  [the longest x13 9.75 us: over_alpha(): lax.ppermute(value, 'alpha', [(i, i ^ flip) for i in range(alpha_devices)])]
    gather x3 -> x8, local copies, waits for them, and re-layouts: 24 us -> 8.76 us  [the longest x2 5.41 us: coupling_matrix(): matrices = patterns[kinds] * coefs[:, :, None, None]]
  transfers between devices with their start and end apart: 3 -> 17, of which waited for: 3 -> 8; matrix products, arithmetic and copies ran while one was open for 34% -> 16% of each run, Pallas kernels for 0% -> 14%
where the time goes in v1:
time: 208 us
  waiting for transfers between devices  118 us (57%)
  local copies, waits for them, and re-layouts  33.9 us (16%)
  Pallas kernels  28.5 us (14%)
  starting transfers between devices  15.2 us (7%)
  matrix products  6.72 us (3%)
  other arithmetic  4.57 us (2%)
    ppermute x13, waiting for transfers between devices, over_alpha(): lax.ppermute(value, 'alpha', [(i, i ^ flip) for i in range(alpha_devices)])  108 us
    pallas_call x4, Pallas kernels, alpha_products(): pl.pallas_call(functools.partial(alpha_kernel, count), grid=(width // til...  14.8 us
    pallas_call x1, Pallas kernels, beta_term(): pl.pallas_call(functools.partial(beta_kernel, layout), in_specs=[smem] *...  13.7 us
    ppermute x4, waiting for transfers between devices, over_beta(): lax.ppermute(value, 'beta', [(i, i ^ flip) for i in range(beta_devices)])  10.8 us
    ppermute x13, starting transfers between devices, over_alpha(): lax.ppermute(value, 'alpha', [(i, i ^ flip) for i in range(alpha_devices)])  9.75 us
    unnamed x39, local copies, waits for them, and re-layouts  8.45 us
    dot_general x2, matrix products, coupling_matrix(): jnp.einsum('osk,ospq->opkq', matches, matrices, precision=lax.Precision.H...  6.72 us
    ppermute x4, starting transfers between devices, over_beta(): lax.ppermute(value, 'beta', [(i, i ^ flip) for i in range(beta_devices)])  5.5 us
  transfers between devices with their start and end apart: 17, of which 8 were waited for; matrix products, arithmetic and copies ran while one was open for 16% of the time, Pallas kernels for 14%

profile of v1, /device:TPU:0, one launch (start us, length us, event | category | flops | bytes accessed | tf_op | source)
XLA Modules:
  0.0 207.6 jit_solution(10837991058570552)
XLA Ops:
  0.0 3.0 %collective-permute-start.10 = (f32[128,6144]{1,0:T(8,128)}, f32[128,6144]{1,0:T(8,128)}, u32[]{:S(2)}, u32[]{:S(2)}) collective-permute-start(f32[128,6144]{1,0:T(8,128)} %refs_0_.9), channel_id=1, source_target_pairs={{0,2},{1,3},{2,0},{3,1},{4,6},{5,7},{6,4},{7,5},{8,10},{9,11},{10,... | collective-permute-start | bytes 9437192 | tf_op jit(solution)/shard_map/ppermute | solution.py:178
  3.0 1.5 collective-permute-start.9
  4.5 3.6 %fusion.16 = (f32[128,1536]{1,0:T(8,128)}, f32[128,1536]{1,0:T(8,128)}, f32[128,1536]{1,0:T(8,128)}, f32[128,1536]{1,0:T(8,128)}) fusion(f32[128,6144]{1,0:T(8,128)} %refs_0_.9), kind=kLoop, calls=%fused_computation.65 | loop fusion | bytes 6291456 | tf_op jit(solution)/shard_map/slice | solution.py:189
  8.1 1.6 collective-permute-start.1
  9.6 0.4 collective-permute-start.3
  10.1 18.6 %collective-permute-done.1.refs_2_ = f32[128,1536]{1,0:T(8,128)} collective-permute-done((f32[128,1536]{1,0:T(8,128)}, f32[128,1536]{1,0:T(8,128)}, u32[]{:S(2)}, u32[]{:S(2)}) %collective-permute-start.1) | collective-permute-done | bytes 786464 | tf_op jit(solution)/shard_map/ppermute | solution.py:175
  28.7 2.6 %collective-permute-start.5 = (f32[128,1536]{1,0:T(8,128)}, f32[128,1536]{1,0:T(8,128)}, u32[]{:S(2)}, u32[]{:S(2)}) collective-permute-start(f32[128,1536]{1,0:T(8,128)} %get-tuple-element.23), channel_id=1, source_target_pairs={{0,16},{4,20},{8,24},{12,28},{16,0},{20,4},{24,8},{28,12},{1,17},{... | collective-permute-start | bytes 2359304 | tf_op jit(solution)/shard_map/ppermute | solution.py:175
  31.5 0.6 gather_fusion
  32.0 0.1 reshape.177
  32.1 28.5 %collective-permute-done.3.refs_2_ = f32[128,1536]{1,0:T(8,128)} collective-permute-done((f32[128,1536]{1,0:T(8,128)}, f32[128,1536]{1,0:T(8,128)}, u32[]{:S(2)}, u32[]{:S(2)}) %collective-permute-start.3) | collective-permute-done | bytes 786464 | tf_op jit(solution)/shard_map/ppermute | solution.py:175
  60.6 10.8 %collective-permute-done.10.refs_2_ = f32[128,6144]{1,0:T(8,128)} collective-permute-done((f32[128,6144]{1,0:T(8,128)}, f32[128,6144]{1,0:T(8,128)}, u32[]{:S(2)}, u32[]{:S(2)}) %collective-permute-start.10) | collective-permute-done | bytes 3145760 | tf_op jit(solution)/shard_map/ppermute | solution.py:178
  71.4 2.7 %slice.40 = f32[64,6144]{1,0:T(8,128)} slice(f32[128,6144]{1,0:T(8,128)} %collective-permute-done.10.refs_2_), slice={[0:64], [0:6144]} | slice | bytes 3145728 | tf_op jit(solution)/shard_map/slice | solution.py:203
  74.1 9.7 %collective-permute-done.5.refs_2_ = f32[128,1536]{1,0:T(8,128)} collective-permute-done((f32[128,1536]{1,0:T(8,128)}, f32[128,1536]{1,0:T(8,128)}, u32[]{:S(2)}, u32[]{:S(2)}) %collective-permute-start.5) | collective-permute-done | bytes 786464 | tf_op jit(solution)/shard_map/ppermute | solution.py:175
  83.8 0.5 collective-permute-start.11
  84.5 0.6 gather_fusion.2
  85.2 0.6 gather_fusion.3
  85.7 0.6 gather_fusion.4
  86.3 2.6 %gather_fusion.1 = f32[32,64,64]{2,1,0:T(8,128)} fusion(f32[16,64,64]{2,1,0:T(8,128)} %param.9, s32[1024]{0:T(1024)S(1)} %pad_clamp_fusion.2), kind=kCustom, calls=%fused_computation.1 | custom fusion | bytes 1048704 | tf_op jit(solution)/shard_map/gather | solution.py:75
  88.9 3.4 %convolution_bitcast_fusion.1 = f32[4,64,8,64]{3,2,1,0:T(8,128)} fusion(f32[4,8,64,64]{3,2,1,0:T(8,128)} %bitcast.46, f32[4,8]{1,0:T(4,128)S(1)} %gather_fusion.2, s32[4,8]{1,0:T(4,128)S(1)} %gather_fusion.3, s32[8]{0:T(128)S(1)} %get-tuple-element.29), kind=kOutput, calls=%fused_computation.11 | convolution fusion | flops 12714240 | bytes 1048864 | tf_op jit(solution)/shard_map/osk,ospq->opkq/dot_general | solution.py:77
  92.3 2.8 %slice.41 = f32[64,6144]{1,0:T(8,128)} slice(f32[128,6144]{1,0:T(8,128)} %collective-permute-done.9.refs_1_), slice={[64:128], [0:6144]} | slice | bytes 3145728 | tf_op jit(solution)/shard_map/slice | solution.py:204
  95.1 4.2 %collective-permute-done.7.refs_2_ = f32[128,1536]{1,0:T(8,128)} collective-permute-done((f32[128,1536]{1,0:T(8,128)}, f32[128,1536]{1,0:T(8,128)}, u32[]{:S(2)}, u32[]{:S(2)}) %collective-permute-start.7) | collective-permute-done | bytes 786464 | tf_op jit(solution)/shard_map/ppermute | solution.py:175
  99.3 0.5 collective-permute-start.12
  99.8 0.8 broadcast_remainder_fusion
  100.6 0.6 gather_fusion.6
  101.2 0.6 gather_fusion.7
  101.7 0.1 copy.28
  101.8 0.1 div.18
  102.0 0.1 copy.27
  102.1 0.1 rem.37
  102.2 1.7 copy-done.2
  103.9 0.2 collective-permute-start.8
  104.1 0.1 sign_compare_fusion
  104.2 0.1 copy.26
  104.3 0.1 ne.40
  104.5 0.1 copy.29
  104.6 0.1 reshape.164.kind_ref
  104.7 2.3 %reshape.161.matrix_ref = f32[256,512]{1,0:T(8,128)} reshape(f32[4,64,8,64]{3,2,1,0:T(8,128)} %convolution_bitcast_fusion.1) | data formatting | bytes 1048576 | tf_op jit(solution)/shard_map/reshape | solution.py:78
  107.0 0.1 reshape.209
  107.1 2.8 %gather_fusion.5 = f32[32,64,64]{2,1,0:T(8,128)} fusion(f32[16,64,64]{2,1,0:T(8,128)} %param.9, s32[1024]{0:T(1024)S(1)} %pad_clamp_fusion), kind=kCustom, calls=%fused_computation.5 | custom fusion | bytes 1048704 | tf_op jit(solution)/shard_map/gather | solution.py:75
  109.9 3.4 %convolution_bitcast_fusion = f32[4,64,8,64]{3,2,1,0:T(8,128)} fusion(f32[4,8,64,64]{3,2,1,0:T(8,128)} %bitcast.45, f32[4,8]{1,0:T(4,128)S(1)} %gather_fusion.6, s32[4,8]{1,0:T(4,128)S(1)} %gather_fusion.7, s32[8]{0:T(128)S(1)} %get-tuple-element.30), kind=kOutput, calls=%fused_computation.10 | convolution fusion | flops 12714240 | bytes 1048864 | tf_op jit(solution)/shard_map/osk,ospq->opkq/dot_general | solution.py:77
  113.2 2.3 %reshape.162.matrix_ref = f32[256,512]{1,0:T(8,128)} reshape(f32[4,64,8,64]{3,2,1,0:T(8,128)} %convolution_bitcast_fusion) | data formatting | bytes 1048576 | tf_op jit(solution)/shard_map/reshape | solution.py:78
  115.5 1.9 copy-done.3
  117.4 1.0 copy-done.5
  118.5 3.7 %shard_map.82 = (f32[128,1536]{1,0:T(8,128)S(1)}, f32[128,1536]{1,0:T(8,128)}) custom-call(f32[256,512]{1,0:T(8,128)S(1)} %copy-done.5, f32[128,6144]{1,0:T(8,128)S(1)} %copy-done.1, f32[128,6144]{1,0:T(8,128)S(1)} %copy-done.3, f32[128,1536]{1,0:T(8,128)} %collective-permute-done.1.refs_2_, f32[128,1536]{1,0:T(8,128)} %collective-permute-done.2.refs_3_), custom_call_target="tpu_custom_call" | custom-call | flops 1207959552 | bytes 4718592 | tf_op jit(solution)/shard_map/pallas_call | solution.py:54
  122.1 0.9 copy-done.6
  123.1 3.8 %shard_map.83 = (f32[128,1536]{1,0:T(8,128)S(1)}, f32[128,1536]{1,0:T(8,128)}) custom-call(f32[256,512]{1,0:T(8,128)S(1)} %copy-done.5, f32[128,6144]{1,0:T(8,128)S(1)} %copy-done.1, f32[128,6144]{1,0:T(8,128)S(1)} %copy-done.3, f32[128,1536]{1,0:T(8,128)} %collective-permute-done.3.refs_2_, f32[128,1536]{1,0:T(8,128)} %collective-permute-done.4.refs_3_), custom_call_target="tpu_custom_call" | custom-call | flops 1207959552 | bytes 4718592 | tf_op jit(solution)/shard_map/pallas_call | solution.py:54
  126.8 0.9 copy-done.8
  127.7 2.9 %collective-permute-start.14 = (f32[128,1536]{1,0:T(8,128)}, f32[128,1536]{1,0:T(8,128)}, u32[]{:S(2)}, u32[]{:S(2)}) collective-permute-start(f32[128,1536]{1,0:T(8,128)} %get-tuple-element.18), channel_id=1, source_target_pairs={{0,16},{4,20},{8,24},{12,28},{16,0},{20,4},{24,8},{28,12},{1,17},{... | collective-permute-start | bytes 2359304 | tf_op jit(solution)/shard_map/ppermute | solution.py:175
  130.6 3.7 %shard_map.84 = (f32[128,1536]{1,0:T(8,128)S(1)}, f32[128,1536]{1,0:T(8,128)}) custom-call(f32[256,512]{1,0:T(8,128)S(1)} %copy-done.4, f32[128,6144]{1,0:T(8,128)S(1)} %copy-done.1, f32[128,6144]{1,0:T(8,128)S(1)} %copy-done.3, f32[128,1536]{1,0:T(8,128)} %collective-permute-done.5.refs_2_, f32[128,1536]{1,0:T(8,128)} %collective-permute-done.6.refs_3_), custom_call_target="tpu_custom_call" | custom-call | flops 1207959552 | bytes 4718592 | tf_op jit(solution)/shard_map/pallas_call | solution.py:54
  134.3 0.9 copy-done.10
  135.2 1.3 collective-permute-start.15
  136.5 3.6 %shard_map.85 = (f32[128,1536]{1,0:T(8,128)S(1)}, f32[128,1536]{1,0:T(8,128)}) custom-call(f32[256,512]{1,0:T(8,128)S(1)} %copy-done.4, f32[128,6144]{1,0:T(8,128)S(1)} %copy-done.1, f32[128,6144]{1,0:T(8,128)S(1)} %copy-done.3, f32[128,1536]{1,0:T(8,128)} %collective-permute-done.7.refs_2_, f32[128,1536]{1,0:T(8,128)} %collective-permute-done.8.refs_3_), custom_call_target="tpu_custom_call" | custom-call | flops 1207959552 | bytes 4718592 | tf_op jit(solution)/shard_map/pallas_call | solution.py:54
  140.1 0.9 copy-done.12
  141.0 0.7 collective-permute-start.16
  141.8 0.1 copy.30
  141.9 0.1 reshape.165.coef_ref
  142.1 1.4 pad_bitcast_fusion.1
  143.5 0.1 pad_maximum_fusion
  143.6 0.1 copy.31
  143.8 13.7 %shard_map.86 = f32[128,6144]{1,0:T(8,128)S(1)} custom-call(s32[1]{0:T(128)} %bitcast.15.me_ref, s32[192]{0:T(256)S(1)} %get-tuple-element.33.slot_ref, s32[192]{0:T(256)S(1)} %get-tuple-element.32.tile_ref, s32[192]{0:T(256)S(1)} %get-tuple-element.31.half_ref, s32[192]{0:T(256)S(1)} %reshape.164.kind_ref, f32[192]{0:T(256)S(1)} %reshape.165.coef_ref, ...), custom_call_target="tpu_custom_call" | custom-call | flops 2415919104 | bytes 15728640 | tf_op jit(solution)/shard_map/pallas_call | solution.py:136
  157.5 20.9 %collective-permute-done.13 = f32[128,1536]{1,0:T(8,128)} collective-permute-done((f32[128,1536]{1,0:T(8,128)}, f32[128,1536]{1,0:T(8,128)}, u32[]{:S(2)}, u32[]{:S(2)}) %collective-permute-start.13) | collective-permute-done | bytes 786464 | tf_op jit(solution)/shard_map/ppermute | solution.py:175
  178.5 16.2 %collective-permute-done.14 = f32[128,1536]{1,0:T(8,128)} collective-permute-done((f32[128,1536]{1,0:T(8,128)}, f32[128,1536]{1,0:T(8,128)}, u32[]{:S(2)}, u32[]{:S(2)}) %collective-permute-start.14) | collective-permute-done | bytes 786464 | tf_op jit(solution)/shard_map/ppermute | solution.py:175
  194.7 9.5 %collective-permute-done.16 = f32[128,1536]{1,0:T(8,128)} collective-permute-done((f32[128,1536]{1,0:T(8,128)}, f32[128,1536]{1,0:T(8,128)}, u32[]{:S(2)}, u32[]{:S(2)}) %collective-permute-start.16) | collective-permute-done | bytes 786464 | tf_op jit(solution)/shard_map/ppermute | solution.py:175
  204.2 3.4 %fusion = f32[128,6144]{1,0:T(8,128)} fusion(f32[128,6144]{1,0:T(8,128)S(1)} %shard_map.86, f32[128,1536]{1,0:T(8,128)S(1)} %copy-done.13, f32[128,1536]{1,0:T(8,128)S(1)} %copy-done.11, f32[128,1536]{1,0:T(8,128)S(1)} %copy-done.9, f32[128,1536]{1,0:T(8,128)S(1)} %copy-done.7, f32[128,1536]{1,0:T(8,128)} %collective-permute-done.16, ...), kind=kLoop, calls=%fused_computation.9 | loop fusion | flops 6291456 | bytes 12582912 | tf_op jit(solution)/shard_map/add | solution.py:241
  (62 shorter events, 0.6 us)
Async XLA Ops:
  0.0 141.8 %copy-start = (f32[384,2]{0,1:T(2,128)S(1)}, f32[384,2]{0,1:T(2,128)}, u32[]{:S(2)}) copy-start(f32[384,2]{0,1:T(2,128)} %param.15) | copy-start | bytes 9220
  0.0 31.4 %copy-start.14 = (s32[16,8]{0,1:T(8,128)S(1)}, s32[16,8]{0,1:T(8,128)}, u32[]{:S(2)}) copy-start(s32[16,8]{0,1:T(8,128)} %param.11) | copy-start | bytes 1540
  0.0 71.4 %collective-permute-start.10 = (f32[128,6144]{1,0:T(8,128)}, f32[128,6144]{1,0:T(8,128)}, u32[]{:S(2)}, u32[]{:S(2)}) collective-permute-start(f32[128,6144]{1,0:T(8,128)} %refs_0_.9), channel_id=1, source_target_pairs={{0,2},{1,3},{2,0},{3,1},{4,6},{5,7},{6,4},{7,5},{8,10},{9,11},{10,... | collective-permute-start | bytes 9437192 | tf_op jit(solution)/shard_map/ppermute | solution.py:178
  3.0 89.3 %collective-permute-start.9 = (f32[128,6144]{1,0:T(8,128)}, f32[128,6144]{1,0:T(8,128)}, u32[]{:S(2)}, u32[]{:S(2)}) collective-permute-start(f32[128,6144]{1,0:T(8,128)} %refs_0_.9), channel_id=1, source_target_pairs={{0,1},{1,0},{2,3},{3,2},{4,5},{5,4},{6,7},{7,6},{8,9},{9,8},{10,11... | collective-permute-start | bytes 9437192 | tf_op jit(solution)/shard_map/ppermute | solution.py:178
  4.5 97.7 %collective-permute-start = (f32[128,6144]{1,0:T(8,128)}, f32[128,6144]{1,0:T(8,128)S(1)}, u32[]{:S(2)}, u32[]{:S(2)}) collective-permute-start(f32[128,6144]{1,0:T(8,128)} %refs_0_.9), channel_id=1, source_target_pairs={{0,4},{4,0},{8,12},{12,8},{16,20},{20,16},{24,28},{28,24},{1,5},{5... | collective-permute-start | bytes 9437192 | tf_op jit(solution)/shard_map/ppermute | solution.py:175
  8.0 76.4 %copy-start.15 = (f32[16,8]{0,1:T(8,128)S(1)}, f32[16,8]{0,1:T(8,128)}, u32[]{:S(2)}) copy-start(f32[16,8]{0,1:T(8,128)} %param.12) | copy-start | bytes 1540
  8.0 77.0 %copy-start.16 = (s32[16,8]{0,1:T(8,128)S(1)}, s32[16,8]{0,1:T(8,128)}, u32[]{:S(2)}) copy-start(s32[16,8]{0,1:T(8,128)} %param.10) | copy-start | bytes 1540
  8.1 20.7 %collective-permute-start.1 = (f32[128,1536]{1,0:T(8,128)}, f32[128,1536]{1,0:T(8,128)}, u32[]{:S(2)}, u32[]{:S(2)}) collective-permute-start(f32[128,1536]{1,0:T(8,128)} %get-tuple-element.21), channel_id=1, source_target_pairs={{0,8},{4,12},{8,0},{12,4},{16,24},{20,28},{24,16},{28,20},{1,9},{5... | collective-permute-start | bytes 2359304 | tf_op jit(solution)/shard_map/ppermute | solution.py:175
  9.6 50.9 %collective-permute-start.3 = (f32[128,1536]{1,0:T(8,128)}, f32[128,1536]{1,0:T(8,128)}, u32[]{:S(2)}, u32[]{:S(2)}) collective-permute-start(f32[128,1536]{1,0:T(8,128)} %get-tuple-element.24), channel_id=1, source_target_pairs={{0,8},{4,12},{8,0},{12,4},{16,24},{20,28},{24,16},{28,20},{1,9},{5... | collective-permute-start | bytes 2359304 | tf_op jit(solution)/shard_map/ppermute | solution.py:175
  28.7 55.1 %collective-permute-start.5 = (f32[128,1536]{1,0:T(8,128)}, f32[128,1536]{1,0:T(8,128)}, u32[]{:S(2)}, u32[]{:S(2)}) collective-permute-start(f32[128,1536]{1,0:T(8,128)} %get-tuple-element.23), channel_id=1, source_target_pairs={{0,16},{4,20},{8,24},{12,28},{16,0},{20,4},{24,8},{28,12},{1,17},{... | collective-permute-start | bytes 2359304 | tf_op jit(solution)/shard_map/ppermute | solution.py:175
  60.6 38.7 %collective-permute-start.7 = (f32[128,1536]{1,0:T(8,128)}, f32[128,1536]{1,0:T(8,128)}, u32[]{:S(2)}, u32[]{:S(2)}) collective-permute-start(f32[128,1536]{1,0:T(8,128)} %get-tuple-element.22), channel_id=1, source_target_pairs={{0,16},{4,20},{8,24},{12,28},{16,0},{20,4},{24,8},{28,12},{1,17},{... | collective-permute-start | bytes 2359304 | tf_op jit(solution)/shard_map/ppermute | solution.py:175
  71.4 27.9 %collective-permute-start.2 = (f32[128,1536]{1,0:T(8,128)}, f32[128,1536]{1,0:T(8,128)}, u32[]{:S(2)}, u32[]{:S(2)}) collective-permute-start(f32[128,1536]{1,0:T(8,128)} %collective-permute-done.1.refs_2_), channel_id=1, source_target_pairs={{0,4},{4,0},{8,12},{12,8},{16,20},{20,16},{24,28},{28,24},{1,5},{5... | collective-permute-start | bytes 2359304 | tf_op jit(solution)/shard_map/ppermute | solution.py:175
  83.8 57.2 %collective-permute-start.11 = (f32[64,6144]{1,0:T(8,128)}, f32[64,6144]{1,0:T(8,128)}, u32[]{:S(2)}, u32[]{:S(2)}) collective-permute-start(f32[64,6144]{1,0:T(8,128)} %slice.40), channel_id=1, source_target_pairs={{0,1},{1,0},{2,3},{3,2},{4,5},{5,4},{6,7},{7,6},{8,9},{9,8},{10,11... | collective-permute-start | bytes 4718600 | tf_op jit(solution)/shard_map/ppermute | solution.py:178
  88.9 10.9 %copy-start.17 = (s32[384,2]{0,1:T(2,128)S(1)}, s32[384,2]{0,1:T(2,128)}, u32[]{:S(2)}) copy-start(s32[384,2]{0,1:T(2,128)} %param.13) | copy-start | bytes 9220
  92.3 30.8 %collective-permute-start.4 = (f32[128,1536]{1,0:T(8,128)}, f32[128,1536]{1,0:T(8,128)}, u32[]{:S(2)}, u32[]{:S(2)}) collective-permute-start(f32[128,1536]{1,0:T(8,128)} %collective-permute-done.3.refs_2_), channel_id=1, source_target_pairs={{0,4},{4,0},{8,12},{12,8},{16,20},{20,16},{24,28},{28,24},{1,5},{5... | collective-permute-start | bytes 2359304 | tf_op jit(solution)/shard_map/ppermute | solution.py:175
  99.3 28.4 %collective-permute-start.6 = (f32[128,1536]{1,0:T(8,128)}, f32[128,1536]{1,0:T(8,128)}, u32[]{:S(2)}, u32[]{:S(2)}) collective-permute-start(f32[128,1536]{1,0:T(8,128)} %collective-permute-done.5.refs_2_), channel_id=1, source_target_pairs={{0,4},{4,0},{8,12},{12,8},{16,20},{20,16},{24,28},{28,24},{1,5},{5... | collective-permute-start | bytes 2359304 | tf_op jit(solution)/shard_map/ppermute | solution.py:175
  99.3 44.4 %collective-permute-start.12 = (f32[64,6144]{1,0:T(8,128)}, f32[64,6144]{1,0:T(8,128)}, u32[]{:S(2)}, u32[]{:S(2)}) collective-permute-start(f32[64,6144]{1,0:T(8,128)} %slice.41), channel_id=1, source_target_pairs={{0,2},{1,3},{2,0},{3,1},{4,6},{5,7},{6,4},{7,5},{8,10},{9,11},{10,... | collective-permute-start | bytes 4718600 | tf_op jit(solution)/shard_map/ppermute | solution.py:178
  102.2 1.7 copy-start.2
  103.9 31.3 %collective-permute-start.8 = (f32[128,1536]{1,0:T(8,128)}, f32[128,1536]{1,0:T(8,128)}, u32[]{:S(2)}, u32[]{:S(2)}) collective-permute-start(f32[128,1536]{1,0:T(8,128)} %collective-permute-done.7.refs_2_), channel_id=1, source_target_pairs={{0,4},{4,0},{8,12},{12,8},{16,20},{20,16},{24,28},{28,24},{1,5},{5... | collective-permute-start | bytes 2359304 | tf_op jit(solution)/shard_map/ppermute | solution.py:175
  107.0 8.5 %copy-start.1 = (f32[128,6144]{1,0:T(8,128)S(1)}, f32[128,6144]{1,0:T(8,128)}, u32[]{:S(2)}) copy-start(f32[128,6144]{1,0:T(8,128)} %refs_0_.9) | copy-start | bytes 9437188
  115.5 1.9 copy-start.3
  117.4 1.0 copy-start.5
  122.1 0.9 copy-start.6
  123.1 7.5 %copy-start.4 = (f32[256,512]{1,0:T(8,128)S(1)}, f32[256,512]{1,0:T(8,128)}, u32[]{:S(2)}) copy-start(f32[256,512]{1,0:T(8,128)} %reshape.162.matrix_ref) | copy-start | bytes 1572868
  123.1 55.4 %collective-permute-start.13 = (f32[128,1536]{1,0:T(8,128)}, f32[128,1536]{1,0:T(8,128)}, u32[]{:S(2)}, u32[]{:S(2)}) collective-permute-start(f32[128,1536]{1,0:T(8,128)} %get-tuple-element.17), channel_id=1, source_target_pairs={{0,16},{4,20},{8,24},{12,28},{16,0},{20,4},{24,8},{28,12},{1,17},{... | collective-permute-start | bytes 2359304 | tf_op jit(solution)/shard_map/ppermute | solution.py:175
  126.8 0.9 copy-start.8
  127.7 67.0 %collective-permute-start.14 = (f32[128,1536]{1,0:T(8,128)}, f32[128,1536]{1,0:T(8,128)}, u32[]{:S(2)}, u32[]{:S(2)}) collective-permute-start(f32[128,1536]{1,0:T(8,128)} %get-tuple-element.18), channel_id=1, source_target_pairs={{0,16},{4,20},{8,24},{12,28},{16,0},{20,4},{24,8},{28,12},{1,17},{... | collective-permute-start | bytes 2359304 | tf_op jit(solution)/shard_map/ppermute | solution.py:175
  134.3 0.9 copy-start.10
  135.2 59.5 %collective-permute-start.15 = (f32[128,1536]{1,0:T(8,128)}, f32[128,1536]{1,0:T(8,128)}, u32[]{:S(2)}, u32[]{:S(2)}) collective-permute-start(f32[128,1536]{1,0:T(8,128)} %get-tuple-element.19), channel_id=1, source_target_pairs={{0,8},{4,12},{8,0},{12,4},{16,24},{20,28},{24,16},{28,20},{1,9},{5... | collective-permute-start | bytes 2359304 | tf_op jit(solution)/shard_map/ppermute | solution.py:175
  140.1 0.9 copy-start.12
  141.0 63.1 %collective-permute-start.16 = (f32[128,1536]{1,0:T(8,128)}, f32[128,1536]{1,0:T(8,128)}, u32[]{:S(2)}, u32[]{:S(2)}) collective-permute-start(f32[128,1536]{1,0:T(8,128)} %get-tuple-element.20), channel_id=1, source_target_pairs={{0,8},{4,12},{8,0},{12,4},{16,24},{20,28},{24,16},{28,20},{1,9},{5... | collective-permute-start | bytes 2359304 | tf_op jit(solution)/shard_map/ppermute | solution.py:175
  143.8 60.4 %copy-start.7 = (f32[128,1536]{1,0:T(8,128)S(1)}, f32[128,1536]{1,0:T(8,128)}, u32[]{:S(2)}) copy-start(f32[128,1536]{1,0:T(8,128)} %copy-done.6) | copy-start | bytes 2359300
  143.8 60.4 %copy-start.9 = (f32[128,1536]{1,0:T(8,128)S(1)}, f32[128,1536]{1,0:T(8,128)}, u32[]{:S(2)}) copy-start(f32[128,1536]{1,0:T(8,128)} %copy-done.8) | copy-start | bytes 2359300
  143.8 60.4 %copy-start.11 = (f32[128,1536]{1,0:T(8,128)S(1)}, f32[128,1536]{1,0:T(8,128)}, u32[]{:S(2)}) copy-start(f32[128,1536]{1,0:T(8,128)} %copy-done.10) | copy-start | bytes 2359300
  143.8 60.4 %copy-start.13 = (f32[128,1536]{1,0:T(8,128)S(1)}, f32[128,1536]{1,0:T(8,128)}, u32[]{:S(2)}) copy-start(f32[128,1536]{1,0:T(8,128)} %copy-done.12) | copy-start | bytes 2359300

commit v2 on v1

v2 whole, which is shorter than its diff:
```python
import functools
import math

import jax
import jax.numpy as jnp
from jax import lax
from jax.experimental import pallas as pl
from jax.experimental.pallas import tpu as pltpu
from jax.sharding import PartitionSpec as P

BLK = 64
LANES = 128


def split(value):
    high = value.astype(jnp.bfloat16)
    low = (value - high.astype(jnp.float32)).astype(jnp.bfloat16)
    return high, low


def dot3(left, right):
    dot = functools.partial(jnp.dot, preferred_element_type=jnp.float32)
    return dot(left[0], right[0]) + (dot(left[0], right[1]) + dot(left[1], right[0]))


def matrix_kernel(weight_ref, side_ref, high_ref, low_ref):
    plans, height, depth = high_ref.shape
    across, down = depth // LANES, height // BLK
    kinds = side_ref.shape[0] // 2

    def pair(index, carry):
        column = lax.rem(index, across)
        line = lax.rem(lax.div(index, across), down)
        plan = lax.div(index, across * down)
        first = index * 2 * kinds
        total = jnp.zeros((BLK, LANES), jnp.float32)
        for side in (0, 1):
            for kind in range(kinds):
                weight = weight_ref[first + side * kinds + kind]
                total = total + weight * side_ref[2 * kind + side]
        high, low = split(total)
        place = (
            plan,
            pl.ds(pl.multiple_of(line * BLK, BLK), BLK),
            pl.ds(pl.multiple_of(column * LANES, LANES), LANES),
        )
        high_ref[place] = high
        low_ref[place] = low
        return carry

    lax.fori_loop(0, plans * across * down, pair, 0)


def coupling_matrices(sides, links, kinds, coefs, targets, sources):
    kind_count = sides.shape[0] // 2
    owner = lax.broadcasted_iota(jnp.int32, links.shape, 0).reshape(-1)
    links, kinds, coefs = links.reshape(-1), kinds.reshape(-1), coefs.reshape(-1)
    at_target = jnp.where(owner == targets[..., None], coefs, 0.0)
    at_source = (links == sources[..., None]).astype(jnp.float32)
    at_kind = kinds == jnp.arange(kind_count, dtype=jnp.int32)[:, None]
    weights = jnp.sum(
        jnp.where(
            at_kind, at_target[:, :, None, None, :] * at_source[:, None, :, None, :], 0.0
        ),
        -1,
    )
    shape = (targets.shape[0], targets.shape[1] * BLK, sources.shape[1] * BLK)
    vmem = pl.BlockSpec(memory_space=pltpu.VMEM)
    return pl.pallas_call(
        matrix_kernel,
        in_specs=[pl.BlockSpec(memory_space=pltpu.SMEM), vmem],
        out_specs=[vmem, vmem],
        out_shape=[jax.ShapeDtypeStruct(shape, jnp.bfloat16)] * 2,
        compiler_params=pltpu.CompilerParams(vmem_limit_bytes=16 * 2**20),
        cost_estimate=pl.CostEstimate(
            flops=2 * kind_count * shape[0] * shape[1] * shape[2],
            bytes_accessed=4 * sides.size,
            transcendentals=0,
        ),
    )(weights.reshape(-1), sides)


def alpha_kernel(count, high_ref, low_ref, *refs):
    piece_refs = refs[:count]
    own_ref, send_ref, piece_high, piece_low = refs[count:]
    rows = own_ref.shape[0]
    for index, piece_ref in enumerate(piece_refs):
        place = pl.ds(index * rows, rows)
        piece_high[place, :], piece_low[place, :] = split(piece_ref[...])
    product = dot3((high_ref[0], low_ref[0]), (piece_high[...], piece_low[...]))
    own_ref[...] = product[:rows]
    send_ref[...] = product[rows:]


def alpha_products(kind, matrices, whole, pieces, start, width):
    rows = whole[0].shape[0]
    tile = math.gcd(math.gcd(start, width), 1024)
    count = len(whole) + len(pieces)
    depth = count * rows
    first = start // tile
    out = jax.ShapeDtypeStruct((rows, width), jnp.float32)
    return pl.pallas_call(
        functools.partial(alpha_kernel, count),
        grid=(width // tile,),
        in_specs=[pl.BlockSpec((1, 2 * rows, depth), lambda i: (kind, 0, 0))] * 2
        + [pl.BlockSpec((rows, tile), lambda i: (0, first + i))] * len(whole)
        + [pl.BlockSpec((rows, tile), lambda i: (0, i))] * len(pieces),
        out_specs=[pl.BlockSpec((rows, tile), lambda i: (0, i))] * 2,
        out_shape=[out, out],
        scratch_shapes=[pltpu.VMEM((depth, tile), jnp.bfloat16)] * 2,
        compiler_params=pltpu.CompilerParams(vmem_limit_bytes=40 * 2**20),
        cost_estimate=pl.CostEstimate(
            flops=12 * rows * depth * width,
            bytes_accessed=4 * (depth + 2 * rows) * width,
            transcendentals=0,
        ),
    )(*matrices, *whole, *pieces)


def add_kernel(starts, total_ref, *refs):
    count = len(starts)
    other_refs, out_ref, held, sums, sems = refs[:count], *refs[count:]
    width = sums.shape[2]
    loads, stores = [], []
    for index, start in enumerate(starts):
        place = pl.ds(start, width)
        loads.append(
            [
                pltpu.make_async_copy(other_refs[index], held.at[index], sems.at[3 * index]),
                pltpu.make_async_copy(
                    total_ref.at[:, place], sums.at[index], sems.at[3 * index + 1]
                ),
            ]
        )
        stores.append(
            pltpu.make_async_copy(
                sums.at[index], out_ref.at[:, place], sems.at[3 * index + 2]
            )
        )
    for pair in loads:
        for copy in pair:
            copy.start()
    for index in range(count):
        for copy in loads[index]:
            copy.wait()
        sums[index] = sums[index] + held[index]
        stores[index].start()
    for copy in stores:
        copy.wait()


def add_at(total, others, starts):
    rows, width = others[0].shape
    count = len(starts)
    anywhere = pl.BlockSpec(memory_space=pl.ANY)
    return pl.pallas_call(
        functools.partial(add_kernel, starts),
        in_specs=[anywhere] * (1 + count),
        out_specs=anywhere,
        out_shape=jax.ShapeDtypeStruct(total.shape, jnp.float32),
        scratch_shapes=[pltpu.VMEM((count, rows, width), jnp.float32)] * 2
        + [pltpu.SemaphoreType.DMA((3 * count,))],
        compiler_params=pltpu.CompilerParams(vmem_limit_bytes=48 * 2**20),
        input_output_aliases={0: 0},
    )(total, *others)


def after(value, *others):
    return lax.optimization_barrier((value, *others))[0]


def beta_kernel(
    layout, me_ref, slot_ref, tile_ref, half_ref, kind_ref, coef_ref, pattern_ref, *refs
):
    parts = refs[: len(layout)]
    out_ref, data, pattern_high, pattern_low, sems = refs[len(layout) :]
    copies = []
    for index, ((flip, row, count), part) in enumerate(zip(layout, parts)):
        slot = lax.bitwise_xor(me_ref[0], flip)
        copies.append(
            pltpu.make_async_copy(part, data.at[slot, pl.ds(row, count)], sems.at[index])
        )
    for copy in copies:
        copy.start()
    pattern_high[...], pattern_low[...] = split(pattern_ref[...])
    for copy in copies:
        copy.wait()
    rows = out_ref.shape[0]
    lower = lax.broadcasted_iota(jnp.int32, (rows, LANES), 1) < BLK

    def block(item, side):
        lanes = pl.ds(pl.multiple_of(tile_ref[item] * LANES, LANES), LANES)
        value = data[slot_ref[item], :, lanes] * coef_ref[item]
        return pltpu.roll(value, BLK * lax.bitwise_xor(half_ref[item], side), 1)

    def pair(index, carry):
        first = index * 4
        left, right = [], []
        for side in (0, 1):
            item = first + 2 * side
            left.append(split(jnp.where(lower, block(item, 0), block(item + 1, 1))))
            for slot in (0, 1):
                kind = kind_ref[item + slot] * 2 + side
                right.append((pattern_high[kind], pattern_low[kind]))
        left = [jnp.concatenate([part[half] for part in left], 1) for half in (0, 1)]
        right = [jnp.concatenate([part[half] for part in right], 0) for half in (0, 1)]
        out_ref[:, pl.ds(pl.multiple_of(index * LANES, LANES), LANES)] = dot3(left, right)
        return carry

    lax.fori_loop(0, out_ref.shape[1] // LANES, pair, 0, unroll=2)


def padded_patterns(patterns):
    zeros = jnp.zeros_like(patterns)
    left = jnp.concatenate([patterns, zeros], 2)
    right = jnp.concatenate([zeros, patterns], 2)
    return jnp.stack([left, right], 1).reshape(-1, BLK, LANES)


def beta_tables(me, own_count, links, kinds, coefs):
    links, kinds, coefs = [
        lax.dynamic_slice_in_dim(array, me * own_count, own_count, 0).reshape(-1)
        for array in (links, kinds, coefs)
    ]
    owner, place = lax.div(links, own_count), lax.rem(links, own_count)
    return owner, lax.div(place, 2), lax.rem(place, 2), kinds, coefs


def beta_term(me, device_count, layout, parts, tables, sides, shape):
    rows, cols = shape
    smem = pl.BlockSpec(memory_space=pltpu.SMEM)
    vmem = pl.BlockSpec(memory_space=pltpu.VMEM)
    return pl.pallas_call(
        functools.partial(beta_kernel, layout),
        in_specs=[smem] * 6 + [vmem] + [pl.BlockSpec(memory_space=pl.ANY)] * len(parts),
        out_specs=vmem,
        out_shape=jax.ShapeDtypeStruct(shape, jnp.float32),
        scratch_shapes=[
            pltpu.VMEM((device_count, rows, cols), jnp.float32),
            pltpu.VMEM(sides.shape, jnp.bfloat16),
            pltpu.VMEM(sides.shape, jnp.bfloat16),
            pltpu.SemaphoreType.DMA((len(parts),)),
        ],
        compiler_params=pltpu.CompilerParams(vmem_limit_bytes=40 * 2**20),
        cost_estimate=pl.CostEstimate(
            flops=12 * rows * cols * 4 * BLK,
            bytes_accessed=4 * rows * cols * (device_count + 1),
            transcendentals=0,
        ),
    )(me.reshape(1), *tables, sides, *parts)


def on_device(
    alpha_devices,
    beta_devices,
    ci_vector,
    patterns,
    alpha_links,
    alpha_kinds,
    alpha_coefs,
    beta_links,
    beta_kinds,
    beta_coefs,
):
    rows, cols = ci_vector.shape
    layers = alpha_devices // 2
    me = lax.axis_index("alpha")
    me_beta = lax.axis_index("beta")

    def over_alpha(value, flip):
        return lax.ppermute(value, "alpha", [(i, i ^ flip) for i in range(alpha_devices)])

    def over_beta(value, flip):
        return lax.ppermute(value, "beta", [(i, i ^ flip) for i in range(beta_devices)])

    plans = [
        ([2 * m for m in range(1, layers // 2)], layers),
        ([4 * m for m in range(1, layers // 2)], 2),
    ]
    width = cols // 4

    def start_of(kind, chunk):
        return (2 * kind + chunk) * width

    peer = over_alpha(ci_vector, 1)
    blocks = rows // BLK
    inner = jnp.arange(blocks, dtype=jnp.int32)
    targets, sources = [], []
    for members, partner in plans:
        flips = [0, 1] + [flip ^ core for flip in members for core in (0, 1)]
        targets.append(
            jnp.concatenate([(me ^ flip) * blocks + inner for flip in (0, partner)])
        )
        sources.append(jnp.concatenate([(me ^ flip) * blocks + inner for flip in flips]))
    sides = after(padded_patterns(patterns), peer)
    matrices = coupling_matrices(
        sides, alpha_links, alpha_kinds, alpha_coefs, jnp.stack(targets), jnp.stack(sources)
    )
    tables = beta_tables(me_beta, cols // BLK, beta_links, beta_kinds, beta_coefs)

    arrived = {}
    for chunk in (0, 1):
        for kind in (1, 0):
            start = start_of(kind, chunk)
            source = after(ci_vector, *arrived[kind, 0]) if chunk else ci_vector
            piece = source[:, start : start + width]
            arrived[kind, chunk] = [over_alpha(piece, flip) for flip in plans[kind][0]]

    def swap(chunk, *earlier):
        swapped = []
        for kind in (0, 1):
            swapped.append([])
            for piece in arrived[kind, chunk]:
                swapped[kind] += [piece, over_alpha(after(piece, *earlier), 1)]
        return swapped

    own, others = {}, {}

    def multiply(chunk, swapped):
        sends = []
        for kind, (_, partner) in enumerate(plans):
            own[kind, chunk], send = alpha_products(
                kind, matrices, [ci_vector, peer], swapped[kind], start_of(kind, chunk), width
            )
            others[kind, chunk] = over_alpha(send, partner)
            sends.append(send)
        return sends

    sends = multiply(0, swap(0, *matrices, *tables))

    whole = after(ci_vector, peer)
    gathered = {0: ci_vector}
    layout, parts = [(0, 0, rows)], [ci_vector]
    for flip in range(1, beta_devices):
        if flip & -flip == flip:
            gathered[flip] = over_beta(whole, flip)
            layout.append((flip, 0, rows))
            parts.append(gathered[flip])
    for flip in range(1, beta_devices):
        low = flip & -flip
        if low != flip:
            first = after(gathered[flip ^ low], *sends)[: rows // 2]
            second = after(gathered[low], *sends)[rows // 2 :]
            top = over_beta(first, low)
            bottom = over_beta(second, flip ^ low)
            gathered[flip] = jnp.concatenate([top, bottom], 0)
            layout += [(flip, 0, rows // 2), (flip, rows // 2, rows // 2)]
            parts += [top, bottom]

    multiply(1, swap(1, *sends))
    total = beta_term(
        me_beta, beta_devices, tuple(layout), parts, tables, sides, (rows, cols)
    )
    total = total + jnp.concatenate(
        [own[kind, chunk] for kind in (0, 1) for chunk in (0, 1)], 1
    )
    for chunk in (0, 1):
        total = add_at(
            total,
            [after(others[kind, chunk], total) for kind in (0, 1)],
            [start_of(kind, chunk) for kind in (0, 1)],
        )
    return total


def solution(mesh):
    return jax.shard_map(
        functools.partial(on_device, mesh.shape["alpha"], mesh.shape["beta"]),
        mesh=mesh,
        in_specs=(P("alpha", "beta"), P(), P(), P(), P(), P(), P(), P()),
        out_specs=P("alpha", "beta"),
        check_vma=False,
    )
```

time: 208 us -> 161 us (0.77)
  waiting for transfers between devices: 118 us -> 89.7 us
  local copies, waits for them, and re-layouts: 33.9 us -> 10.4 us
  Pallas kernels: 28.5 us -> 35.4 us
  matrix products: 6.72 us -> 0 us
  starting transfers between devices: 15.2 us -> 21.5 us
    ppermute x13, waiting for transfers between devices: 108 us -> 44.1 us  [over_alpha(): lax.ppermute(value, 'alpha', [(i, i ^ flip) for i in range(alpha_devices)])]
    ppermute x4, waiting for transfers between devices: 10.8 us -> 45.6 us  [over_beta(): lax.ppermute(value, 'beta', [(i, i ^ flip) for i in range(beta_devices)])]
    gather x8 -> x0, local copies, waits for them, and re-layouts: 8.76 us -> none  [the longest x2 5.41 us: coupling_matrix(): matrices = patterns[kinds] * coefs[:, :, None, None]]
    pallas_call x0 -> x3, Pallas kernels: none -> 8.75 us  [the longest x2 4.91 us: add_at(): pl.pallas_call(functools.partial(add_kernel, starts), in_specs=[anywhere]...]
    unnamed x39 -> x13, local copies, waits for them, and re-layouts: 8.45 us -> 0.23 us
    dot_general x2 -> x0, matrix products: 6.72 us -> none  [coupling_matrix(): jnp.einsum('osk,ospq->opkq', matches, matrices, precision=lax.Precision.H...]
    ppermute x13, starting transfers between devices: 9.75 us -> 15.4 us  [over_alpha(): lax.ppermute(value, 'alpha', [(i, i ^ flip) for i in range(alpha_devices)])]
    reshape x4, local copies, waits for them, and re-layouts: 4.87 us -> 0.43 us  [the longest x2 0.27 us: beta_tables(): lax.dynamic_slice_in_dim(array, me * own_count, own_count, 0).reshape(-1)]
  transfers between devices with their start and end apart: 17 -> 17, of which waited for: 8 -> 7; matrix products, arithmetic and copies ran while one was open for 16% -> 9% of each run, Pallas kernels for 14% -> 20%
where the time goes in v2:
time: 161 us
  waiting for transfers between devices  89.7 us (56%)
  Pallas kernels  35.4 us (22%)
  starting transfers between devices  21.5 us (13%)
  local copies, waits for them, and re-layouts  10.4 us (6%)
  other arithmetic  3.46 us (2%)
    ppermute x4, waiting for transfers between devices, over_beta(): lax.ppermute(value, 'beta', [(i, i ^ flip) for i in range(beta_devices)])  45.6 us
    ppermute x13, waiting for transfers between devices, over_alpha(): lax.ppermute(value, 'alpha', [(i, i ^ flip) for i in range(alpha_devices)])  44.1 us
    ppermute x13, starting transfers between devices, over_alpha(): lax.ppermute(value, 'alpha', [(i, i ^ flip) for i in range(alpha_devices)])  15.4 us
    pallas_call x4, Pallas kernels, alpha_products(): pl.pallas_call(functools.partial(alpha_kernel, count), grid=(width // til...  13.8 us
    pallas_call x1, Pallas kernels, beta_term(): pl.pallas_call(functools.partial(beta_kernel, layout), in_specs=[smem] *...  12.8 us
    ppermute x4, starting transfers between devices, over_beta(): lax.ppermute(value, 'beta', [(i, i ^ flip) for i in range(beta_devices)])  6.15 us
    pallas_call x2, Pallas kernels, add_at(): pl.pallas_call(functools.partial(add_kernel, starts), in_specs=[anywhere]...  4.91 us
    pallas_call x1, Pallas kernels, coupling_matrices(): pl.pallas_call(matrix_kernel, in_specs=[pl.BlockSpec(memory_space=pltpu.S...  3.83 us
  transfers between devices with their start and end apart: 17, of which 7 were waited for; matrix products, arithmetic and copies ran while one was open for 9% of the time, Pallas kernels for 20%

profile of v2, /device:TPU:0, one launch (start us, length us, event | category | flops | bytes accessed | tf_op | source)
XLA Modules:
  0.0 160.7 jit_solution(2398355216007061171)
XLA Ops:
  0.0 0.5 collective-permute-start
  0.5 2.9 %fusion.2 = (f32[128,1536]{1,0:T(8,128)}, f32[128,1536]{1,0:T(8,128)}) fusion(f32[128,6144]{1,0:T(8,128)} %refs_0_.9), kind=kLoop, calls=%fused_computation.31 | loop fusion | bytes 3145728 | tf_op jit(solution)/shard_map/slice | solution.py:306
  3.4 3.5 %collective-permute-start.5 = (f32[128,1536]{1,0:T(8,128)}, f32[128,1536]{1,0:T(8,128)}, u32[]{:S(2)}, u32[]{:S(2)}) collective-permute-start(f32[128,1536]{1,0:T(8,128)} %get-tuple-element.53), channel_id=1, source_target_pairs={{0,16},{4,20},{8,24},{12,28},{16,0},{20,4},{24,8},{28,12},{1,17},{... | collective-permute-start | bytes 2359304 | tf_op jit(solution)/shard_map/ppermute | solution.py:271
  6.9 1.6 collective-permute-start.3
  8.5 1.6 collective-permute-start.2
  10.1 1.5 collective-permute-start.1
  11.6 0.1 add_bitcast_fusion
  11.7 0.1 copy.30
  11.8 0.1 eq.61
  11.9 0.1 copy.28
  11.9 0.1 eq.53
  12.0 0.1 copy.29
  12.1 0.1 reshape.42
  12.2 0.1 eq.57
  12.3 0.1 add_bitcast_fusion.2
  12.4 0.1 compare_select_fusion
  12.5 0.1 compare_convert_fusion
  12.6 0.2 select_reduce_fusion
  12.8 0.1 reshape.43.weight_ref
  12.9 0.8 fusion
  13.6 0.1 copy.24
  13.7 0.1 rem.16
  13.9 0.1 constant_dynamic-slice_fusion
  14.0 0.1 copy.26
  14.1 0.1 reshape.40.coef_ref
  14.2 0.1 copy.23
  14.3 0.1 div.21.slot_ref
  14.5 0.1 copy.25
  14.6 0.1 reshape.39.kind_ref
  14.7 1.4 pad_bitcast_fusion.1
  16.1 0.1 pad_maximum_fusion
  16.3 0.1 copy.27
  16.4 3.8 %shard_map.82 = (bf16[2,256,512]{2,1,0:T(8,128)(2,1)S(1)}, bf16[2,256,512]{2,1,0:T(8,128)(2,1)S(1)}) custom-call(f32[1024]{0:T(1024)S(1)} %reshape.43.weight_ref, f32[32,64,128]{2,1,0:T(8,128)S(1)} %bitcast.16), custom_call_target="tpu_custom_call" | custom-call | flops 8388608 | bytes 1048576 | tf_op jit(solution)/shard_map/pallas_call | solution.py:69
  20.2 22.4 %collective-permute-done.3.refs_2_ = f32[128,1536]{1,0:T(8,128)} collective-permute-done((f32[128,1536]{1,0:T(8,128)}, f32[128,1536]{1,0:T(8,128)}, u32[]{:S(2)}, u32[]{:S(2)}) %collective-permute-start.3) | collective-permute-done | bytes 786464 | tf_op jit(solution)/shard_map/ppermute | solution.py:271
  42.7 0.0 collective-permute-start.4
  42.7 0.0 collective-permute-done.5.refs_2_
  42.7 0.5 collective-permute-start.6
  43.2 0.1 slice.23
  43.2 1.4 collective-permute-start.11
  44.7 0.1 slice.22
  44.8 0.4 collective-permute-done.4.refs_3_
  45.2 1.7 %collective-permute-start.9 = (f32[128,1536]{1,0:T(8,128)S(1)}, f32[128,1536]{1,0:T(8,128)S(1)}, u32[]{:S(2)}, u32[]{:S(2)}) collective-permute-start(f32[128,1536]{1,0:T(8,128)S(1)} %slice.22), channel_id=1, source_target_pairs={{0,8},{4,12},{8,0},{12,4},{16,24},{20,28},{24,16},{28,20},{1,9},{5... | collective-permute-start | bytes 2359304 | tf_op jit(solution)/shard_map/ppermute | solution.py:271
  46.8 3.3 %shard_map.83 = (f32[128,1536]{1,0:T(8,128)S(1)}, f32[128,1536]{1,0:T(8,128)S(1)}) custom-call(bf16[2,256,512]{2,1,0:T(8,128)(2,1)S(1)} %get-tuple-element.31.high_ref, bf16[2,256,512]{2,1,0:T(8,128)(2,1)S(1)} %get-tuple-element.32.low_ref, f32[128,6144]{1,0:T(8,128)S(1)} %copy-done.1, f32[128,6144]{1,0:T(8,128)} %collective-permute-done.refs_1_, ...), custom_call_target="tpu_custom_call" | custom-call | flops 1207959552 | bytes 4718592 | tf_op jit(solution)/shard_map/pallas_call | solution.py:102
  50.2 3.4 %shard_map.84 = (f32[128,1536]{1,0:T(8,128)S(1)}, f32[128,1536]{1,0:T(8,128)S(1)}) custom-call(bf16[2,256,512]{2,1,0:T(8,128)(2,1)S(1)} %get-tuple-element.31.high_ref, bf16[2,256,512]{2,1,0:T(8,128)(2,1)S(1)} %get-tuple-element.32.low_ref, f32[128,6144]{1,0:T(8,128)S(1)} %copy-done.1, f32[128,6144]{1,0:T(8,128)} %collective-permute-done.refs_1_, ...), custom_call_target="tpu_custom_call" | custom-call | flops 1207959552 | bytes 4718592 | tf_op jit(solution)/shard_map/pallas_call | solution.py:102
  53.6 25.1 %collective-permute-done.2.refs_2_ = f32[128,6144]{1,0:T(8,128)} collective-permute-done((f32[128,6144]{1,0:T(8,128)S(1)}, f32[128,6144]{1,0:T(8,128)}, u32[]{:S(2)}, u32[]{:S(2)}) %collective-permute-start.2) | collective-permute-done | bytes 3145760 | tf_op jit(solution)/shard_map/ppermute | solution.py:274
  78.7 1.5 slice.20
  80.2 1.6 collective-permute-start.7
  81.8 2.7 %slice.21 = f32[64,6144]{1,0:T(8,128)} slice(f32[128,6144]{1,0:T(8,128)} %collective-permute-done.1.refs_1_), slice={[64:128], [0:6144]} | slice | bytes 3145728 | tf_op jit(solution)/shard_map/slice | solution.py:343
  84.5 1.5 collective-permute-start.8
  86.0 0.5 collective-permute-start.12
  86.5 1.7 %collective-permute-start.13 = (f32[128,1536]{1,0:T(8,128)S(1)}, f32[128,1536]{1,0:T(8,128)S(1)}, u32[]{:S(2)}, u32[]{:S(2)}) collective-permute-start(f32[128,1536]{1,0:T(8,128)S(1)} %get-tuple-element.34), channel_id=1, source_target_pairs={{0,16},{4,20},{8,24},{12,28},{16,0},{20,4},{24,8},{28,12},{1,17},{... | collective-permute-start | bytes 2359304 | tf_op jit(solution)/shard_map/ppermute | solution.py:271
  88.2 0.1 collective-permute-done.10.refs_3_
  88.3 1.5 collective-permute-start.14
  89.8 3.9 %shard_map.86 = (f32[128,1536]{1,0:T(8,128)S(1)}, f32[128,1536]{1,0:T(8,128)}) custom-call(bf16[2,256,512]{2,1,0:T(8,128)(2,1)S(1)} %get-tuple-element.31.high_ref, bf16[2,256,512]{2,1,0:T(8,128)(2,1)S(1)} %get-tuple-element.32.low_ref, f32[128,6144]{1,0:T(8,128)S(1)} %copy-done.1, f32[128,6144]{1,0:T(8,128)} %collective-permute-done.refs_1_, ...), custom_call_target="tpu_custom_call" | custom-call | flops 1207959552 | bytes 4718592 | tf_op jit(solution)/shard_map/pallas_call | solution.py:102
  93.7 1.8 %collective-permute-start.15 = (f32[128,1536]{1,0:T(8,128)}, f32[128,1536]{1,0:T(8,128)S(1)}, u32[]{:S(2)}, u32[]{:S(2)}) collective-permute-start(f32[128,1536]{1,0:T(8,128)} %get-tuple-element.49), channel_id=1, source_target_pairs={{0,16},{4,20},{8,24},{12,28},{16,0},{20,4},{24,8},{28,12},{1,17},{... | collective-permute-start | bytes 2359304 | tf_op jit(solution)/shard_map/ppermute | solution.py:271
  95.4 3.2 %shard_map.87 = (f32[128,1536]{1,0:T(8,128)S(1)}, f32[128,1536]{1,0:T(8,128)S(1)}) custom-call(bf16[2,256,512]{2,1,0:T(8,128)(2,1)S(1)} %get-tuple-element.31.high_ref, bf16[2,256,512]{2,1,0:T(8,128)(2,1)S(1)} %get-tuple-element.32.low_ref, f32[128,6144]{1,0:T(8,128)S(1)} %copy-done.1, f32[128,6144]{1,0:T(8,128)} %collective-permute-done.refs_1_, ...), custom_call_target="tpu_custom_call" | custom-call | flops 1207959552 | bytes 4718592 | tf_op jit(solution)/shard_map/pallas_call | solution.py:102
  98.7 17.1 %collective-permute-done.7.refs_3_ = f32[64,6144]{1,0:T(8,128)S(1)} collective-permute-done((f32[64,6144]{1,0:T(8,128)S(1)}, f32[64,6144]{1,0:T(8,128)S(1)}, u32[]{:S(2)}, u32[]{:S(2)}) %collective-permute-start.7) | collective-permute-done | bytes 1572896 | tf_op jit(solution)/shard_map/ppermute | solution.py:274
  115.8 0.8 collective-permute-start.16
  116.6 3.3 %collective-permute-done.8.refs_4_ = f32[64,6144]{1,0:T(8,128)S(1)} collective-permute-done((f32[64,6144]{1,0:T(8,128)}, f32[64,6144]{1,0:T(8,128)S(1)}, u32[]{:S(2)}, u32[]{:S(2)}) %collective-permute-start.8) | collective-permute-done | bytes 1572896 | tf_op jit(solution)/shard_map/ppermute | solution.py:274
  119.9 12.8 %shard_map.85 = f32[128,6144]{1,0:T(8,128)S(1)} custom-call(s32[1]{0:T(128)} %bitcast.me_ref, s32[192]{0:T(256)S(1)} %div.21.slot_ref, s32[192]{0:T(256)S(1)} %get-tuple-element.62.tile_ref, s32[192]{0:T(256)S(1)} %get-tuple-element.61.half_ref, s32[192]{0:T(256)S(1)} %reshape.39.kind_ref, f32[192]{0:T(256)S(1)} %reshape.40.coef_ref, ...), custom_call_target="tpu_custom_call" | custom-call | flops 2415919104 | bytes 15728640 | tf_op jit(solution)/shard_map/pallas_call | solution.py:233
  132.7 2.0 %maximum_add_fusion.total_ref = f32[128,6144]{1,0:T(8,128)} fusion(f32[128,6144]{1,0:T(8,128)S(1)} %shard_map.85, f32[128,1536]{1,0:T(8,128)S(1)} %get-tuple-element.46, f32[128,1536]{1,0:T(8,128)S(1)} %get-tuple-element.43, f32[128,1536]{1,0:T(8,128)S(1)} %get-tuple-element.42, f32[128,1536]{1,0:T(8,128)S(1)} %get-tuple-element.39), kind=kLoop, calls=%fused_computation | loop fusion | flops 3145728 | bytes 9437184 | tf_op jit(solution)/shard_map/add | solution.py:354
  134.7 2.5 %shard_map.88.total_ref = f32[128,6144]{1,0:T(8,128)} custom-call(f32[128,6144]{1,0:T(8,128)} %maximum_add_fusion.total_ref, f32[128,1536]{1,0:T(8,128)S(1)} %collective-permute-done.13.refs_0_, f32[128,1536]{1,0:T(8,128)S(1)} %collective-permute-done.14.refs_1_), custom_call_target="tpu_custom_call", output_to_operand_aliasing={{}: (0, {})} | custom-call | tf_op jit(solution)/shard_map/pallas_call | solution.py:156
  137.1 21.1 %collective-permute-done.16.refs_1_ = f32[128,1536]{1,0:T(8,128)S(1)} collective-permute-done((f32[128,1536]{1,0:T(8,128)S(1)}, f32[128,1536]{1,0:T(8,128)S(1)}, u32[]{:S(2)}, u32[]{:S(2)}) %collective-permute-start.16) | collective-permute-done | bytes 786464 | tf_op jit(solution)/shard_map/ppermute | solution.py:271
  158.2 2.5 %shard_map.89 = f32[128,6144]{1,0:T(8,128)} custom-call(f32[128,6144]{1,0:T(8,128)} %shard_map.88.total_ref, f32[128,1536]{1,0:T(8,128)S(1)} %collective-permute-done.15.refs_0_, f32[128,1536]{1,0:T(8,128)S(1)} %collective-permute-done.16.refs_1_), custom_call_target="tpu_custom_call", output_to_operand_aliasing={{}: (0, {})} | custom-call | tf_op jit(solution)/shard_map/pallas_call | solution.py:156
  (29 shorter events, 0.1 us)
Async XLA Ops:
  0.0 13.9 %copy-start = (f32[384,2]{0,1:T(2,128)S(1)}, f32[384,2]{0,1:T(2,128)}, u32[]{:S(2)}) copy-start(f32[384,2]{0,1:T(2,128)} %param.15) | copy-start | bytes 9220
  0.0 8.5 %copy-start.1 = (f32[128,6144]{1,0:T(8,128)S(1)}, f32[128,6144]{1,0:T(8,128)}, u32[]{:S(2)}) copy-start(f32[128,6144]{1,0:T(8,128)} %refs_0_.9) | copy-start | bytes 9437188
  0.0 11.7 %copy-start.2 = (s32[16,8]{0,1:T(8,128)S(1)}, s32[16,8]{0,1:T(8,128)}, u32[]{:S(2)}) copy-start(s32[16,8]{0,1:T(8,128)} %param.10) | copy-start | bytes 1540
  0.0 11.8 %copy-start.3 = (s32[16,8]{0,1:T(8,128)S(1)}, s32[16,8]{0,1:T(8,128)}, u32[]{:S(2)}) copy-start(s32[16,8]{0,1:T(8,128)} %param.11) | copy-start | bytes 1540
  0.0 12.0 %copy-start.4 = (f32[16,8]{0,1:T(8,128)S(1)}, f32[16,8]{0,1:T(8,128)}, u32[]{:S(2)}) copy-start(f32[16,8]{0,1:T(8,128)} %param.12) | copy-start | bytes 1540
  0.0 8.5 %collective-permute-start = (f32[128,6144]{1,0:T(8,128)}, f32[128,6144]{1,0:T(8,128)}, u32[]{:S(2)}, u32[]{:S(2)}) collective-permute-start(f32[128,6144]{1,0:T(8,128)} %refs_0_.9), channel_id=1, source_target_pairs={{0,4},{4,0},{8,12},{12,8},{16,20},{20,16},{24,28},{28,24},{1,5},{5... | collective-permute-start | bytes 9437192 | tf_op jit(solution)/shard_map/ppermute | solution.py:271
  3.4 39.2 %collective-permute-start.5 = (f32[128,1536]{1,0:T(8,128)}, f32[128,1536]{1,0:T(8,128)}, u32[]{:S(2)}, u32[]{:S(2)}) collective-permute-start(f32[128,1536]{1,0:T(8,128)} %get-tuple-element.53), channel_id=1, source_target_pairs={{0,16},{4,20},{8,24},{12,28},{16,0},{20,4},{24,8},{28,12},{1,17},{... | collective-permute-start | bytes 2359304 | tf_op jit(solution)/shard_map/ppermute | solution.py:271
  6.9 35.7 %collective-permute-start.3 = (f32[128,1536]{1,0:T(8,128)}, f32[128,1536]{1,0:T(8,128)}, u32[]{:S(2)}, u32[]{:S(2)}) collective-permute-start(f32[128,1536]{1,0:T(8,128)} %get-tuple-element.54), channel_id=1, source_target_pairs={{0,8},{4,12},{8,0},{12,4},{16,24},{20,28},{24,16},{28,20},{1,9},{5... | collective-permute-start | bytes 2359304 | tf_op jit(solution)/shard_map/ppermute | solution.py:271
  8.5 70.2 %collective-permute-start.2 = (f32[128,6144]{1,0:T(8,128)S(1)}, f32[128,6144]{1,0:T(8,128)}, u32[]{:S(2)}, u32[]{:S(2)}) collective-permute-start(f32[128,6144]{1,0:T(8,128)S(1)} %copy-done.1), channel_id=1, source_target_pairs={{0,2},{1,3},{2,0},{3,1},{4,6},{5,7},{6,4},{7,5},{8,10},{9,11},{10,... | collective-permute-start | bytes 9437192 | tf_op jit(solution)/shard_map/ppermute | solution.py:274
  10.1 71.7 %collective-permute-start.1 = (f32[128,6144]{1,0:T(8,128)S(1)}, f32[128,6144]{1,0:T(8,128)}, u32[]{:S(2)}, u32[]{:S(2)}) collective-permute-start(f32[128,6144]{1,0:T(8,128)S(1)} %copy-done.1), channel_id=1, source_target_pairs={{0,1},{1,0},{2,3},{3,2},{4,5},{5,4},{6,7},{7,6},{8,9},{9,8},{10,11... | collective-permute-start | bytes 9437192 | tf_op jit(solution)/shard_map/ppermute | solution.py:274
  42.7 2.5 %collective-permute-start.4 = (f32[128,1536]{1,0:T(8,128)}, f32[128,1536]{1,0:T(8,128)S(1)}, u32[]{:S(2)}, u32[]{:S(2)}) collective-permute-start(f32[128,1536]{1,0:T(8,128)} %collective-permute-done.3.refs_2_), channel_id=1, source_target_pairs={{0,4},{4,0},{8,12},{12,8},{16,20},{20,16},{24,28},{28,24},{1,5},{5... | collective-permute-start | bytes 2359304 | tf_op jit(solution)/shard_map/ppermute | solution.py:271
  42.7 7.5 %collective-permute-start.6 = (f32[128,1536]{1,0:T(8,128)}, f32[128,1536]{1,0:T(8,128)S(1)}, u32[]{:S(2)}, u32[]{:S(2)}) collective-permute-start(f32[128,1536]{1,0:T(8,128)} %collective-permute-done.5.refs_2_), channel_id=1, source_target_pairs={{0,4},{4,0},{8,12},{12,8},{16,20},{20,16},{24,28},{28,24},{1,5},{5... | collective-permute-start | bytes 2359304 | tf_op jit(solution)/shard_map/ppermute | solution.py:271
  43.2 42.8 %collective-permute-start.11 = (f32[128,1536]{1,0:T(8,128)S(1)}, f32[128,1536]{1,0:T(8,128)S(1)}, u32[]{:S(2)}, u32[]{:S(2)}) collective-permute-start(f32[128,1536]{1,0:T(8,128)S(1)} %slice.23), channel_id=1, source_target_pairs={{0,16},{4,20},{8,24},{12,28},{16,0},{20,4},{24,8},{28,12},{1,17},{... | collective-permute-start | bytes 2359304 | tf_op jit(solution)/shard_map/ppermute | solution.py:271
  45.2 40.8 %collective-permute-start.9 = (f32[128,1536]{1,0:T(8,128)S(1)}, f32[128,1536]{1,0:T(8,128)S(1)}, u32[]{:S(2)}, u32[]{:S(2)}) collective-permute-start(f32[128,1536]{1,0:T(8,128)S(1)} %slice.22), channel_id=1, source_target_pairs={{0,8},{4,12},{8,0},{12,4},{16,24},{20,28},{24,16},{28,20},{1,9},{5... | collective-permute-start | bytes 2359304 | tf_op jit(solution)/shard_map/ppermute | solution.py:271
  80.2 35.5 %collective-permute-start.7 = (f32[64,6144]{1,0:T(8,128)S(1)}, f32[64,6144]{1,0:T(8,128)S(1)}, u32[]{:S(2)}, u32[]{:S(2)}) collective-permute-start(f32[64,6144]{1,0:T(8,128)S(1)} %slice.20), channel_id=1, source_target_pairs={{0,1},{1,0},{2,3},{3,2},{4,5},{5,4},{6,7},{7,6},{8,9},{9,8},{10,11... | collective-permute-start | bytes 4718600 | tf_op jit(solution)/shard_map/ppermute | solution.py:274
  84.5 35.4 %collective-permute-start.8 = (f32[64,6144]{1,0:T(8,128)}, f32[64,6144]{1,0:T(8,128)S(1)}, u32[]{:S(2)}, u32[]{:S(2)}) collective-permute-start(f32[64,6144]{1,0:T(8,128)} %slice.21), channel_id=1, source_target_pairs={{0,2},{1,3},{2,0},{3,1},{4,6},{5,7},{6,4},{7,5},{8,10},{9,11},{10,... | collective-permute-start | bytes 4718600 | tf_op jit(solution)/shard_map/ppermute | solution.py:274
  86.0 2.3 %collective-permute-start.10 = (f32[128,1536]{1,0:T(8,128)S(1)}, f32[128,1536]{1,0:T(8,128)S(1)}, u32[]{:S(2)}, u32[]{:S(2)}) collective-permute-start(f32[128,1536]{1,0:T(8,128)S(1)} %collective-permute-done.9.refs_2_), channel_id=1, source_target_pairs={{0,4},{4,0},{8,12},{12,8},{16,20},{20,16},{24,28},{28,24},{1,5},{5... | collective-permute-start | bytes 2359304 | tf_op jit(solution)/shard_map/ppermute | solution.py:271
  86.0 7.7 %collective-permute-start.12 = (f32[128,1536]{1,0:T(8,128)S(1)}, f32[128,1536]{1,0:T(8,128)S(1)}, u32[]{:S(2)}, u32[]{:S(2)}) collective-permute-start(f32[128,1536]{1,0:T(8,128)S(1)} %collective-permute-done.11.refs_2_), channel_id=1, source_target_pairs={{0,4},{4,0},{8,12},{12,8},{16,20},{20,16},{24,28},{28,24},{1,5},{5... | collective-permute-start | bytes 2359304 | tf_op jit(solution)/shard_map/ppermute | solution.py:271
  86.5 48.2 %collective-permute-start.13 = (f32[128,1536]{1,0:T(8,128)S(1)}, f32[128,1536]{1,0:T(8,128)S(1)}, u32[]{:S(2)}, u32[]{:S(2)}) collective-permute-start(f32[128,1536]{1,0:T(8,128)S(1)} %get-tuple-element.34), channel_id=1, source_target_pairs={{0,16},{4,20},{8,24},{12,28},{16,0},{20,4},{24,8},{28,12},{1,17},{... | collective-permute-start | bytes 2359304 | tf_op jit(solution)/shard_map/ppermute | solution.py:271
  88.3 46.4 %collective-permute-start.14 = (f32[128,1536]{1,0:T(8,128)S(1)}, f32[128,1536]{1,0:T(8,128)S(1)}, u32[]{:S(2)}, u32[]{:S(2)}) collective-permute-start(f32[128,1536]{1,0:T(8,128)S(1)} %get-tuple-element.36), channel_id=1, source_target_pairs={{0,8},{4,12},{8,0},{12,4},{16,24},{20,28},{24,16},{28,20},{1,9},{5... | collective-permute-start | bytes 2359304 | tf_op jit(solution)/shard_map/ppermute | solution.py:271
  93.7 64.6 %collective-permute-start.15 = (f32[128,1536]{1,0:T(8,128)}, f32[128,1536]{1,0:T(8,128)S(1)}, u32[]{:S(2)}, u32[]{:S(2)}) collective-permute-start(f32[128,1536]{1,0:T(8,128)} %get-tuple-element.49), channel_id=1, source_target_pairs={{0,16},{4,20},{8,24},{12,28},{16,0},{20,4},{24,8},{28,12},{1,17},{... | collective-permute-start | bytes 2359304 | tf_op jit(solution)/shard_map/ppermute | solution.py:271
  115.8 42.5 %collective-permute-start.16 = (f32[128,1536]{1,0:T(8,128)S(1)}, f32[128,1536]{1,0:T(8,128)S(1)}, u32[]{:S(2)}, u32[]{:S(2)}) collective-permute-start(f32[128,1536]{1,0:T(8,128)S(1)} %get-tuple-element.51), channel_id=1, source_target_pairs={{0,8},{4,12},{8,0},{12,4},{16,24},{20,28},{24,16},{28,20},{1,9},{5... | collective-permute-start | bytes 2359304 | tf_op jit(solution)/shard_map/ppermute | solution.py:271

commit v3 on v2

--- a/solution.py
+++ b/solution.py
@@ -10,6 +10,7 @@
 
 BLK = 64
 LANES = 128
+SPLITS = 4
 
 
 def split(value):
@@ -117,6 +118,53 @@
     )(*matrices, *whole, *pieces)
 
 
+def take_kernel(places, source_count, *refs):
+    source_refs, (*out_refs, held, sems) = refs[:source_count], refs[source_count:]
+    loads, stores = [], []
+    for number, ((index, row, start), out_ref) in enumerate(zip(places, out_refs)):
+        rows, width = out_ref.shape
+        step = rows // SPLITS
+        for part in range(SPLITS):
+            place = pl.ds(part * step, step)
+            loads.append(
+                pltpu.make_async_copy(
+                    source_refs[index].at[pl.ds(row + part * step, step), pl.ds(start, width)],
+                    held.at[number, place],
+                    sems.at[0, len(loads)],
+                )
+            )
+            stores.append(
+                pltpu.make_async_copy(
+                    held.at[number, place], out_ref.at[place], sems.at[1, len(stores)]
+                )
+            )
+    for load in loads:
+        load.start()
+    for load, store in zip(loads, stores):
+        load.wait()
+        store.start()
+    for store in stores:
+        store.wait()
+
+
+def take(sources, places, shapes, limit=16):
+    anywhere = pl.BlockSpec(memory_space=pl.ANY)
+    return pl.pallas_call(
+        functools.partial(take_kernel, tuple(places), len(sources)),
+        in_specs=[anywhere] * len(sources),
+        out_specs=[anywhere] * len(places),
+        out_shape=[jax.ShapeDtypeStruct(shape, jnp.float32) for shape in shapes],
+        scratch_shapes=[
+            pltpu.VMEM((len(places), *shapes[0]), jnp.float32),
+            pltpu.SemaphoreType.DMA((2, SPLITS * len(places))),
+        ],
+        compiler_params=pltpu.CompilerParams(vmem_limit_bytes=limit * 2**20),
+        cost_estimate=pl.CostEstimate(
+            flops=0, bytes_accessed=sum(8 * a * b for a, b in shapes), transcendentals=0
+        ),
+    )(*sources)
+
+
 def add_kernel(starts, total_ref, *refs):
     count = len(starts)
     other_refs, out_ref, held, sums, sems = refs[:count], *refs[count:]
@@ -299,11 +347,17 @@
     tables = beta_tables(me_beta, cols // BLK, beta_links, beta_kinds, beta_coefs)
 
     arrived = {}
+    pieces = take(
+        [ci_vector], [(0, 0, start_of(kind, 0)) for kind in (1, 0)], [(rows, width)] * 2, 56
+    )
+    pieces += take(
+        [after(ci_vector, *matrices)],
+        [(0, 0, start_of(kind, 1)) for kind in (1, 0)],
+        [(rows, width)] * 2,
+    )
     for chunk in (0, 1):
         for kind in (1, 0):
-            start = start_of(kind, chunk)
-            source = after(ci_vector, *arrived[kind, 0]) if chunk else ci_vector
-            piece = source[:, start : start + width]
+            piece = pieces[2 * chunk + 1 - kind]
             arrived[kind, chunk] = [over_alpha(piece, flip) for flip in plans[kind][0]]
 
     def swap(chunk, *earlier):
@@ -326,7 +380,7 @@
             sends.append(send)
         return sends
 
-    sends = multiply(0, swap(0, *matrices, *tables))
+    sends = multiply(0, swap(0, *matrices, *tables, *pieces[2:]))
 
     whole = after(ci_vector, peer)
     gathered = {0: ci_vector}
@@ -339,8 +393,11 @@
     for flip in range(1, beta_devices):
         low = flip & -flip
         if low != flip:
-            first = after(gathered[flip ^ low], *sends)[: rows // 2]
-            second = after(gathered[low], *sends)[rows // 2 :]
+            first, second = take(
+                [after(gathered[flip ^ low], *sends), gathered[low]],
+                [(0, 0, 0), (1, rows // 2, 0)],
+                [(rows // 2, cols)] * 2,
+            )
             top = over_beta(first, low)
             bottom = over_beta(second, flip ^ low)
             gathered[flip] = jnp.concatenate([top, bottom], 0)

time: 161 us -> 159 us (0.988)
  Pallas kernels: 35.4 us -> 43.7 us
  local copies, waits for them, and re-layouts: 10.4 us -> 3.24 us
  waiting for transfers between devices: 89.7 us -> 87.6 us
    pallas_call x0 -> x3, Pallas kernels: none -> 7.63 us  [take(): pl.pallas_call(functools.partial(take_kernel, tuple(places), len(sources)...]
    slice x5 -> x0, local copies, waits for them, and re-layouts: 7.19 us -> none  [the longest x3 3.01 us: on_device(): piece = source[:, start:start + width]]
    ppermute x13, waiting for transfers between devices: 44.1 us -> 40.2 us  [over_alpha(): lax.ppermute(value, 'alpha', [(i, i ^ flip) for i in range(alpha_devices)])]
    ppermute x4, waiting for transfers between devices: 45.6 us -> 47.4 us  [over_beta(): lax.ppermute(value, 'beta', [(i, i ^ flip) for i in range(beta_devices)])]
  transfers between devices with their start and end apart: 17 -> 17, of which waited for: 7 -> 7; matrix products, arithmetic and copies ran while one was open for 9% -> 4% of each run, Pallas kernels for 20% -> 26%
where the time goes in v3:
time: 159 us
  waiting for transfers between devices  87.6 us (55%)
  Pallas kernels  43.7 us (27%)
  starting transfers between devices  20.3 us (13%)
  other arithmetic  3.46 us (2%)
  local copies, waits for them, and re-layouts  3.24 us (2%)
    ppermute x4, waiting for transfers between devices, over_beta(): lax.ppermute(value, 'beta', [(i, i ^ flip) for i in range(beta_devices)])  47.4 us
    ppermute x13, waiting for transfers between devices, over_alpha(): lax.ppermute(value, 'alpha', [(i, i ^ flip) for i in range(alpha_devices)])  40.2 us
    ppermute x13, starting transfers between devices, over_alpha(): lax.ppermute(value, 'alpha', [(i, i ^ flip) for i in range(alpha_devices)])  15.2 us
    pallas_call x4, Pallas kernels, alpha_products(): pl.pallas_call(functools.partial(alpha_kernel, count), grid=(width // til...  14.6 us
    pallas_call x1, Pallas kernels, beta_term(): pl.pallas_call(functools.partial(beta_kernel, layout), in_specs=[smem] *...  12.8 us
    pallas_call x3, Pallas kernels, take(): pl.pallas_call(functools.partial(take_kernel, tuple(places), len(sources)...  7.63 us
    ppermute x4, starting transfers between devices, over_beta(): lax.ppermute(value, 'beta', [(i, i ^ flip) for i in range(beta_devices)])  5.14 us
    pallas_call x2, Pallas kernels, add_at(): pl.pallas_call(functools.partial(add_kernel, starts), in_specs=[anywhere]...  4.91 us
  transfers between devices with their start and end apart: 17, of which 7 were waited for; matrix products, arithmetic and copies ran while one was open for 4% of the time, Pallas kernels for 26%

profile of v3, /device:TPU:0, one launch (start us, length us, event | category | flops | bytes accessed | tf_op | source)
XLA Modules:
  0.0 158.6 jit_solution(9640795714009165907)
XLA Ops:
  0.0 0.5 collective-permute-start
  0.5 2.6 %shard_map.83 = (f32[128,1536]{1,0:T(8,128)}, f32[128,1536]{1,0:T(8,128)}) custom-call(f32[128,6144]{1,0:T(8,128)} %refs_0_.12), custom_call_target="tpu_custom_call" | custom-call | bytes 3145728 | tf_op jit(solution)/shard_map/pallas_call | solution.py:152
  3.1 2.5 %collective-permute-start.3 = (f32[128,1536]{1,0:T(8,128)}, f32[128,1536]{1,0:T(8,128)}, u32[]{:S(2)}, u32[]{:S(2)}) collective-permute-start(f32[128,1536]{1,0:T(8,128)} %get-tuple-element.37), channel_id=1, source_target_pairs={{0,8},{4,12},{8,0},{12,4},{16,24},{20,28},{24,16},{28,20},{1,9},{5... | collective-permute-start | bytes 2359304 | tf_op jit(solution)/shard_map/ppermute | solution.py:319
  5.7 2.6 %collective-permute-start.5 = (f32[128,1536]{1,0:T(8,128)}, f32[128,1536]{1,0:T(8,128)}, u32[]{:S(2)}, u32[]{:S(2)}) collective-permute-start(f32[128,1536]{1,0:T(8,128)} %get-tuple-element.43), channel_id=1, source_target_pairs={{0,16},{4,20},{8,24},{12,28},{16,0},{20,4},{24,8},{28,12},{1,17},{... | collective-permute-start | bytes 2359304 | tf_op jit(solution)/shard_map/ppermute | solution.py:319
  8.3 1.6 collective-permute-start.2
  9.9 1.5 collective-permute-start.1
  11.4 0.1 add_bitcast_fusion
  11.4 0.1 copy.30
  11.5 0.1 eq.61
  11.6 0.1 copy.28
  11.7 0.1 eq.53
  11.8 0.1 copy.29
  11.8 0.1 reshape.42
  11.9 0.1 eq.57
  12.1 0.1 add_bitcast_fusion.2
  12.2 0.1 compare_select_fusion
  12.2 0.1 compare_convert_fusion
  12.3 0.2 select_reduce_fusion
  12.5 0.1 reshape.43.weight_ref
  12.6 0.8 fusion
  13.4 0.1 copy.24
  13.5 0.1 rem.16
  13.6 0.1 constant_dynamic-slice_fusion
  13.7 0.1 copy.26
  13.8 0.1 reshape.40.coef_ref
  14.0 0.1 copy.23
  14.1 0.1 div.21.slot_ref
  14.2 0.1 copy.25
  14.3 0.1 reshape.39.kind_ref
  14.5 1.4 pad_bitcast_fusion.1
  15.9 0.1 pad_maximum_fusion
  16.0 0.1 copy.27
  16.1 3.8 %shard_map.82 = (bf16[2,256,512]{2,1,0:T(8,128)(2,1)S(1)}, bf16[2,256,512]{2,1,0:T(8,128)(2,1)S(1)}) custom-call(f32[1024]{0:T(1024)S(1)} %reshape.43.weight_ref, f32[32,64,128]{2,1,0:T(8,128)S(1)} %bitcast.16), custom_call_target="tpu_custom_call" | custom-call | flops 8388608 | bytes 1048576 | tf_op jit(solution)/shard_map/pallas_call | solution.py:70
  20.0 2.7 %shard_map.84 = (f32[128,1536]{1,0:T(8,128)S(1)}, f32[128,1536]{1,0:T(8,128)S(1)}) custom-call(f32[128,6144]{1,0:T(8,128)S(1)} %copy-done.1), custom_call_target="tpu_custom_call" | custom-call | bytes 3145728 | tf_op jit(solution)/shard_map/pallas_call | solution.py:152
  22.7 18.3 %collective-permute-done.3.refs_2_ = f32[128,1536]{1,0:T(8,128)} collective-permute-done((f32[128,1536]{1,0:T(8,128)}, f32[128,1536]{1,0:T(8,128)}, u32[]{:S(2)}, u32[]{:S(2)}) %collective-permute-start.3) | collective-permute-done | bytes 786464 | tf_op jit(solution)/shard_map/ppermute | solution.py:319
  41.0 0.0 collective-permute-start.4
  41.0 2.5 %collective-permute-done.5.refs_2_ = f32[128,1536]{1,0:T(8,128)} collective-permute-done((f32[128,1536]{1,0:T(8,128)}, f32[128,1536]{1,0:T(8,128)}, u32[]{:S(2)}, u32[]{:S(2)}) %collective-permute-start.5) | collective-permute-done | bytes 786464 | tf_op jit(solution)/shard_map/ppermute | solution.py:319
  43.5 0.3 collective-permute-start.11
  43.9 2.7 %collective-permute-start.9 = (f32[128,1536]{1,0:T(8,128)S(1)}, f32[128,1536]{1,0:T(8,128)S(1)}, u32[]{:S(2)}, u32[]{:S(2)}) collective-permute-start(f32[128,1536]{1,0:T(8,128)S(1)} %get-tuple-element.40), channel_id=1, source_target_pairs={{0,8},{4,12},{8,0},{12,4},{16,24},{20,28},{24,16},{28,20},{1,9},{5... | collective-permute-start | bytes 2359304 | tf_op jit(solution)/shard_map/ppermute | solution.py:319
  46.6 3.3 %shard_map.85 = (f32[128,1536]{1,0:T(8,128)S(1)}, f32[128,1536]{1,0:T(8,128)S(1)}) custom-call(bf16[2,256,512]{2,1,0:T(8,128)(2,1)S(1)} %get-tuple-element.35.high_ref, bf16[2,256,512]{2,1,0:T(8,128)(2,1)S(1)} %get-tuple-element.36.low_ref, f32[128,6144]{1,0:T(8,128)S(1)} %copy-done.1, f32[128,6144]{1,0:T(8,128)} %collective-permute-done.refs_1_, ...), custom_call_target="tpu_custom_call" | custom-call | flops 1207959552 | bytes 4718592 | tf_op jit(solution)/shard_map/pallas_call | solution.py:103
  49.9 0.0 collective-permute-done.6.refs_3_
  49.9 3.4 %shard_map.86 = (f32[128,1536]{1,0:T(8,128)S(1)}, f32[128,1536]{1,0:T(8,128)S(1)}) custom-call(bf16[2,256,512]{2,1,0:T(8,128)(2,1)S(1)} %get-tuple-element.35.high_ref, bf16[2,256,512]{2,1,0:T(8,128)(2,1)S(1)} %get-tuple-element.36.low_ref, f32[128,6144]{1,0:T(8,128)S(1)} %copy-done.1, f32[128,6144]{1,0:T(8,128)} %collective-permute-done.refs_1_, ...), custom_call_target="tpu_custom_call" | custom-call | flops 1207959552 | bytes 4718592 | tf_op jit(solution)/shard_map/pallas_call | solution.py:103
  53.3 25.2 %collective-permute-done.2.refs_0_.refs_2_ = f32[128,6144]{1,0:T(8,128)} collective-permute-done((f32[128,6144]{1,0:T(8,128)S(1)}, f32[128,6144]{1,0:T(8,128)}, u32[]{:S(2)}, u32[]{:S(2)}) %collective-permute-start.2) | collective-permute-done | bytes 3145760 | tf_op jit(solution)/shard_map/ppermute | solution.py:322
  78.5 1.2 collective-permute-done.1.refs_1_
  79.7 2.4 %shard_map.87 = (f32[64,6144]{1,0:T(8,128)}, f32[64,6144]{1,0:T(8,128)S(1)}) custom-call(f32[128,6144]{1,0:T(8,128)} %collective-permute-done.2.refs_0_.refs_2_, f32[128,6144]{1,0:T(8,128)} %collective-permute-done.1.refs_1_), custom_call_target="tpu_custom_call" | custom-call | bytes 6291456 | tf_op jit(solution)/shard_map/pallas_call | solution.py:152
  82.1 1.6 collective-permute-start.7
  83.6 0.5 collective-permute-start.8
  84.2 0.0 collective-permute-done.11.refs_2_
  84.2 0.0 collective-permute-start.12
  84.2 0.0 collective-permute-done.9.refs_2_
  84.2 0.5 collective-permute-start.10
  84.7 1.9 %collective-permute-start.13 = (f32[128,1536]{1,0:T(8,128)S(1)}, f32[128,1536]{1,0:T(8,128)S(1)}, u32[]{:S(2)}, u32[]{:S(2)}) collective-permute-start(f32[128,1536]{1,0:T(8,128)S(1)} %get-tuple-element.42), channel_id=1, source_target_pairs={{0,16},{4,20},{8,24},{12,28},{16,0},{20,4},{24,8},{28,12},{1,17},{... | collective-permute-start | bytes 2359304 | tf_op jit(solution)/shard_map/ppermute | solution.py:319
  86.6 1.6 collective-permute-start.14
  88.2 4.0 %shard_map.90 = (f32[128,1536]{1,0:T(8,128)S(1)}, f32[128,1536]{1,0:T(8,128)}) custom-call(bf16[2,256,512]{2,1,0:T(8,128)(2,1)S(1)} %get-tuple-element.35.high_ref, bf16[2,256,512]{2,1,0:T(8,128)(2,1)S(1)} %get-tuple-element.36.low_ref, f32[128,6144]{1,0:T(8,128)S(1)} %copy-done.1, f32[128,6144]{1,0:T(8,128)} %collective-permute-done.refs_1_, ...), custom_call_target="tpu_custom_call" | custom-call | flops 1207959552 | bytes 4718592 | tf_op jit(solution)/shard_map/pallas_call | solution.py:103
  92.1 0.4 collective-permute-start.16
  92.6 3.9 %shard_map.89 = (f32[128,1536]{1,0:T(8,128)S(1)}, f32[128,1536]{1,0:T(8,128)}) custom-call(bf16[2,256,512]{2,1,0:T(8,128)(2,1)S(1)} %get-tuple-element.35.high_ref, bf16[2,256,512]{2,1,0:T(8,128)(2,1)S(1)} %get-tuple-element.36.low_ref, f32[128,6144]{1,0:T(8,128)S(1)} %copy-done.1, f32[128,6144]{1,0:T(8,128)} %collective-permute-done.refs_1_, ...), custom_call_target="tpu_custom_call" | custom-call | flops 1207959552 | bytes 4718592 | tf_op jit(solution)/shard_map/pallas_call | solution.py:103
  96.5 21.0 %collective-permute-done.7.refs_3_ = f32[64,6144]{1,0:T(8,128)S(1)} collective-permute-done((f32[64,6144]{1,0:T(8,128)}, f32[64,6144]{1,0:T(8,128)S(1)}, u32[]{:S(2)}, u32[]{:S(2)}) %collective-permute-start.7) | collective-permute-done | bytes 1572896 | tf_op jit(solution)/shard_map/ppermute | solution.py:322
  117.5 2.0 %collective-permute-start.15 = (f32[128,1536]{1,0:T(8,128)}, f32[128,1536]{1,0:T(8,128)S(1)}, u32[]{:S(2)}, u32[]{:S(2)}) collective-permute-start(f32[128,1536]{1,0:T(8,128)} %get-tuple-element.57), channel_id=1, source_target_pairs={{0,16},{4,20},{8,24},{12,28},{16,0},{20,4},{24,8},{28,12},{1,17},{... | collective-permute-start | bytes 2359304 | tf_op jit(solution)/shard_map/ppermute | solution.py:319
  119.6 12.8 %shard_map.88 = f32[128,6144]{1,0:T(8,128)S(1)} custom-call(s32[1]{0:T(128)} %bitcast.me_ref, s32[192]{0:T(256)S(1)} %div.21.slot_ref, s32[192]{0:T(256)S(1)} %get-tuple-element.68.tile_ref, s32[192]{0:T(256)S(1)} %get-tuple-element.67.half_ref, s32[192]{0:T(256)S(1)} %reshape.39.kind_ref, f32[192]{0:T(256)S(1)} %reshape.40.coef_ref, ...), custom_call_target="tpu_custom_call" | custom-call | flops 2415919104 | bytes 15728640 | tf_op jit(solution)/shard_map/pallas_call | solution.py:281
  132.3 2.0 %maximum_add_fusion.total_ref = f32[128,6144]{1,0:T(8,128)} fusion(f32[128,6144]{1,0:T(8,128)S(1)} %shard_map.88, f32[128,1536]{1,0:T(8,128)S(1)} %get-tuple-element.54, f32[128,1536]{1,0:T(8,128)S(1)} %get-tuple-element.52, f32[128,1536]{1,0:T(8,128)S(1)} %get-tuple-element.51, f32[128,1536]{1,0:T(8,128)S(1)} %get-tuple-element.49), kind=kLoop, calls=%fused_computation | loop fusion | flops 3145728 | bytes 9437184 | tf_op jit(solution)/shard_map/add | solution.py:411
  134.4 5.9 %collective-permute-done.14.refs_1_ = f32[128,1536]{1,0:T(8,128)S(1)} collective-permute-done((f32[128,1536]{1,0:T(8,128)S(1)}, f32[128,1536]{1,0:T(8,128)S(1)}, u32[]{:S(2)}, u32[]{:S(2)}) %collective-permute-start.14) | collective-permute-done | bytes 786464 | tf_op jit(solution)/shard_map/ppermute | solution.py:319
  140.3 2.5 %shard_map.91.total_ref = f32[128,6144]{1,0:T(8,128)} custom-call(f32[128,6144]{1,0:T(8,128)} %maximum_add_fusion.total_ref, f32[128,1536]{1,0:T(8,128)S(1)} %collective-permute-done.13.refs_0_, f32[128,1536]{1,0:T(8,128)S(1)} %collective-permute-done.14.refs_1_), custom_call_target="tpu_custom_call", output_to_operand_aliasing={{}: (0, {})} | custom-call | tf_op jit(solution)/shard_map/pallas_call | solution.py:204
  142.7 13.4 %collective-permute-done.16.refs_1_ = f32[128,1536]{1,0:T(8,128)S(1)} collective-permute-done((f32[128,1536]{1,0:T(8,128)}, f32[128,1536]{1,0:T(8,128)S(1)}, u32[]{:S(2)}, u32[]{:S(2)}) %collective-permute-start.16) | collective-permute-done | bytes 786464 | tf_op jit(solution)/shard_map/ppermute | solution.py:319
  156.1 2.5 %shard_map.92 = f32[128,6144]{1,0:T(8,128)} custom-call(f32[128,6144]{1,0:T(8,128)} %shard_map.91.total_ref, f32[128,1536]{1,0:T(8,128)S(1)} %collective-permute-done.15.refs_0_, f32[128,1536]{1,0:T(8,128)S(1)} %collective-permute-done.16.refs_1_), custom_call_target="tpu_custom_call", output_to_operand_aliasing={{}: (0, {})} | custom-call | tf_op jit(solution)/shard_map/pallas_call | solution.py:204
  (27 shorter events, 0.1 us)
Async XLA Ops:
  0.0 13.6 %copy-start = (f32[384,2]{0,1:T(2,128)S(1)}, f32[384,2]{0,1:T(2,128)}, u32[]{:S(2)}) copy-start(f32[384,2]{0,1:T(2,128)} %param.15) | copy-start | bytes 9220
  0.0 8.3 %copy-start.1 = (f32[128,6144]{1,0:T(8,128)S(1)}, f32[128,6144]{1,0:T(8,128)}, u32[]{:S(2)}) copy-start(f32[128,6144]{1,0:T(8,128)} %refs_0_.12) | copy-start | bytes 9437188
  0.0 11.4 %copy-start.2 = (s32[16,8]{0,1:T(8,128)S(1)}, s32[16,8]{0,1:T(8,128)}, u32[]{:S(2)}) copy-start(s32[16,8]{0,1:T(8,128)} %param.10) | copy-start | bytes 1540
  0.0 11.6 %copy-start.3 = (s32[16,8]{0,1:T(8,128)S(1)}, s32[16,8]{0,1:T(8,128)}, u32[]{:S(2)}) copy-start(s32[16,8]{0,1:T(8,128)} %param.11) | copy-start | bytes 1540
  0.0 11.8 %copy-start.4 = (f32[16,8]{0,1:T(8,128)S(1)}, f32[16,8]{0,1:T(8,128)}, u32[]{:S(2)}) copy-start(f32[16,8]{0,1:T(8,128)} %param.12) | copy-start | bytes 1540
  0.0 8.2 %collective-permute-start = (f32[128,6144]{1,0:T(8,128)}, f32[128,6144]{1,0:T(8,128)}, u32[]{:S(2)}, u32[]{:S(2)}) collective-permute-start(f32[128,6144]{1,0:T(8,128)} %refs_0_.12), channel_id=1, source_target_pairs={{0,4},{4,0},{8,12},{12,8},{16,20},{20,16},{24,28},{28,24},{1,5},{5... | collective-permute-start | bytes 9437192 | tf_op jit(solution)/shard_map/ppermute | solution.py:319
  3.1 37.9 %collective-permute-start.3 = (f32[128,1536]{1,0:T(8,128)}, f32[128,1536]{1,0:T(8,128)}, u32[]{:S(2)}, u32[]{:S(2)}) collective-permute-start(f32[128,1536]{1,0:T(8,128)} %get-tuple-element.37), channel_id=1, source_target_pairs={{0,8},{4,12},{8,0},{12,4},{16,24},{20,28},{24,16},{28,20},{1,9},{5... | collective-permute-start | bytes 2359304 | tf_op jit(solution)/shard_map/ppermute | solution.py:319
  5.7 37.9 %collective-permute-start.5 = (f32[128,1536]{1,0:T(8,128)}, f32[128,1536]{1,0:T(8,128)}, u32[]{:S(2)}, u32[]{:S(2)}) collective-permute-start(f32[128,1536]{1,0:T(8,128)} %get-tuple-element.43), channel_id=1, source_target_pairs={{0,16},{4,20},{8,24},{12,28},{16,0},{20,4},{24,8},{28,12},{1,17},{... | collective-permute-start | bytes 2359304 | tf_op jit(solution)/shard_map/ppermute | solution.py:319
  8.3 70.2 %collective-permute-start.2 = (f32[128,6144]{1,0:T(8,128)S(1)}, f32[128,6144]{1,0:T(8,128)}, u32[]{:S(2)}, u32[]{:S(2)}) collective-permute-start(f32[128,6144]{1,0:T(8,128)S(1)} %copy-done.1), channel_id=1, source_target_pairs={{0,2},{1,3},{2,0},{3,1},{4,6},{5,7},{6,4},{7,5},{8,10},{9,11},{10,... | collective-permute-start | bytes 9437192 | tf_op jit(solution)/shard_map/ppermute | solution.py:322
  9.9 69.9 %collective-permute-start.1 = (f32[128,6144]{1,0:T(8,128)S(1)}, f32[128,6144]{1,0:T(8,128)}, u32[]{:S(2)}, u32[]{:S(2)}) collective-permute-start(f32[128,6144]{1,0:T(8,128)S(1)} %copy-done.1), channel_id=1, source_target_pairs={{0,1},{1,0},{2,3},{3,2},{4,5},{5,4},{6,7},{7,6},{8,9},{9,8},{10,11... | collective-permute-start | bytes 9437192 | tf_op jit(solution)/shard_map/ppermute | solution.py:322
  41.0 2.9 %collective-permute-start.4 = (f32[128,1536]{1,0:T(8,128)}, f32[128,1536]{1,0:T(8,128)S(1)}, u32[]{:S(2)}, u32[]{:S(2)}) collective-permute-start(f32[128,1536]{1,0:T(8,128)} %collective-permute-done.3.refs_2_), channel_id=1, source_target_pairs={{0,4},{4,0},{8,12},{12,8},{16,20},{20,16},{24,28},{28,24},{1,5},{5... | collective-permute-start | bytes 2359304 | tf_op jit(solution)/shard_map/ppermute | solution.py:319
  43.5 6.4 %collective-permute-start.6 = (f32[128,1536]{1,0:T(8,128)}, f32[128,1536]{1,0:T(8,128)S(1)}, u32[]{:S(2)}, u32[]{:S(2)}) collective-permute-start(f32[128,1536]{1,0:T(8,128)} %collective-permute-done.5.refs_2_), channel_id=1, source_target_pairs={{0,4},{4,0},{8,12},{12,8},{16,20},{20,16},{24,28},{28,24},{1,5},{5... | collective-permute-start | bytes 2359304 | tf_op jit(solution)/shard_map/ppermute | solution.py:319
  43.5 40.6 %collective-permute-start.11 = (f32[128,1536]{1,0:T(8,128)S(1)}, f32[128,1536]{1,0:T(8,128)S(1)}, u32[]{:S(2)}, u32[]{:S(2)}) collective-permute-start(f32[128,1536]{1,0:T(8,128)S(1)} %get-tuple-element.39), channel_id=1, source_target_pairs={{0,16},{4,20},{8,24},{12,28},{16,0},{20,4},{24,8},{28,12},{1,17},{... | collective-permute-start | bytes 2359304 | tf_op jit(solution)/shard_map/ppermute | solution.py:319
  43.9 40.3 %collective-permute-start.9 = (f32[128,1536]{1,0:T(8,128)S(1)}, f32[128,1536]{1,0:T(8,128)S(1)}, u32[]{:S(2)}, u32[]{:S(2)}) collective-permute-start(f32[128,1536]{1,0:T(8,128)S(1)} %get-tuple-element.40), channel_id=1, source_target_pairs={{0,8},{4,12},{8,0},{12,4},{16,24},{20,28},{24,16},{28,20},{1,9},{5... | collective-permute-start | bytes 2359304 | tf_op jit(solution)/shard_map/ppermute | solution.py:319
  82.1 35.4 %collective-permute-start.7 = (f32[64,6144]{1,0:T(8,128)}, f32[64,6144]{1,0:T(8,128)S(1)}, u32[]{:S(2)}, u32[]{:S(2)}) collective-permute-start(f32[64,6144]{1,0:T(8,128)} %get-tuple-element.47), channel_id=1, source_target_pairs={{0,1},{1,0},{2,3},{3,2},{4,5},{5,4},{6,7},{7,6},{8,9},{9,8},{10,11... | collective-permute-start | bytes 4718600 | tf_op jit(solution)/shard_map/ppermute | solution.py:322
  83.6 35.9 %collective-permute-start.8 = (f32[64,6144]{1,0:T(8,128)S(1)}, f32[64,6144]{1,0:T(8,128)S(1)}, u32[]{:S(2)}, u32[]{:S(2)}) collective-permute-start(f32[64,6144]{1,0:T(8,128)S(1)} %get-tuple-element.48), channel_id=1, source_target_pairs={{0,2},{1,3},{2,0},{3,1},{4,6},{5,7},{6,4},{7,5},{8,10},{9,11},{10,... | collective-permute-start | bytes 4718600 | tf_op jit(solution)/shard_map/ppermute | solution.py:322
  84.2 2.4 %collective-permute-start.12 = (f32[128,1536]{1,0:T(8,128)S(1)}, f32[128,1536]{1,0:T(8,128)S(1)}, u32[]{:S(2)}, u32[]{:S(2)}) collective-permute-start(f32[128,1536]{1,0:T(8,128)S(1)} %collective-permute-done.11.refs_2_), channel_id=1, source_target_pairs={{0,4},{4,0},{8,12},{12,8},{16,20},{20,16},{24,28},{28,24},{1,5},{5... | collective-permute-start | bytes 2359304 | tf_op jit(solution)/shard_map/ppermute | solution.py:319
  84.2 8.0 %collective-permute-start.10 = (f32[128,1536]{1,0:T(8,128)S(1)}, f32[128,1536]{1,0:T(8,128)S(1)}, u32[]{:S(2)}, u32[]{:S(2)}) collective-permute-start(f32[128,1536]{1,0:T(8,128)S(1)} %collective-permute-done.9.refs_2_), channel_id=1, source_target_pairs={{0,4},{4,0},{8,12},{12,8},{16,20},{20,16},{24,28},{28,24},{1,5},{5... | collective-permute-start | bytes 2359304 | tf_op jit(solution)/shard_map/ppermute | solution.py:319
  84.7 55.6 %collective-permute-start.13 = (f32[128,1536]{1,0:T(8,128)S(1)}, f32[128,1536]{1,0:T(8,128)S(1)}, u32[]{:S(2)}, u32[]{:S(2)}) collective-permute-start(f32[128,1536]{1,0:T(8,128)S(1)} %get-tuple-element.42), channel_id=1, source_target_pairs={{0,16},{4,20},{8,24},{12,28},{16,0},{20,4},{24,8},{28,12},{1,17},{... | collective-permute-start | bytes 2359304 | tf_op jit(solution)/shard_map/ppermute | solution.py:319
  86.6 53.7 %collective-permute-start.14 = (f32[128,1536]{1,0:T(8,128)S(1)}, f32[128,1536]{1,0:T(8,128)S(1)}, u32[]{:S(2)}, u32[]{:S(2)}) collective-permute-start(f32[128,1536]{1,0:T(8,128)S(1)} %get-tuple-element.45), channel_id=1, source_target_pairs={{0,8},{4,12},{8,0},{12,4},{16,24},{20,28},{24,16},{28,20},{1,9},{5... | collective-permute-start | bytes 2359304 | tf_op jit(solution)/shard_map/ppermute | solution.py:319
  92.1 64.0 %collective-permute-start.16 = (f32[128,1536]{1,0:T(8,128)}, f32[128,1536]{1,0:T(8,128)S(1)}, u32[]{:S(2)}, u32[]{:S(2)}) collective-permute-start(f32[128,1536]{1,0:T(8,128)} %get-tuple-element.59), channel_id=1, source_target_pairs={{0,8},{4,12},{8,0},{12,4},{16,24},{20,28},{24,16},{28,20},{1,9},{5... | collective-permute-start | bytes 2359304 | tf_op jit(solution)/shard_map/ppermute | solution.py:319
  117.5 38.6 %collective-permute-start.15 = (f32[128,1536]{1,0:T(8,128)}, f32[128,1536]{1,0:T(8,128)S(1)}, u32[]{:S(2)}, u32[]{:S(2)}) collective-permute-start(f32[128,1536]{1,0:T(8,128)} %get-tuple-element.57), channel_id=1, source_target_pairs={{0,16},{4,20},{8,24},{12,28},{16,0},{20,4},{24,8},{28,12},{1,17},{... | collective-permute-start | bytes 2359304 | tf_op jit(solution)/shard_map/ppermute | solution.py:319

commit v4 on v3

--- a/solution.py
+++ b/solution.py
@@ -211,6 +211,49 @@
         compiler_params=pltpu.CompilerParams(vmem_limit_bytes=48 * 2**20),
         input_output_aliases={0: 0},
     )(total, *others)
+
+
+def last_kernel(starts, *refs):
+    count = len(starts)
+    other_refs, base_refs = refs[1 : 1 + count], refs[1 + count : 1 + 2 * count]
+    out_ref, held, sems = refs[1 + 2 * count :]
+    width = held.shape[2]
+    loads, stores = [], []
+    for index, start in enumerate(starts):
+        loads.append(
+            pltpu.make_async_copy(other_refs[index], held.at[index], sems.at[2 * index])
+        )
+        stores.append(
+            pltpu.make_async_copy(
+                held.at[index], out_ref.at[:, pl.ds(start, width)], sems.at[2 * index + 1]
+            )
+        )
+    for load in loads:
+        load.start()
+    for index in range(count):
+        loads[index].wait()
+        held[index] = held[index] + base_refs[index][...]
+        stores[index].start()
+    for store in stores:
+        store.wait()
+
+
+def add_last(total, bases, others, starts):
+    rows, width = others[0].shape
+    count = len(starts)
+    anywhere = pl.BlockSpec(memory_space=pl.ANY)
+    return pl.pallas_call(
+        functools.partial(last_kernel, starts),
+        in_specs=[anywhere] * (1 + count) + [pl.BlockSpec(memory_space=pltpu.VMEM)] * count,
+        out_specs=anywhere,
+        out_shape=jax.ShapeDtypeStruct(total.shape, jnp.float32),
+        scratch_shapes=[
+            pltpu.VMEM((count, rows, width), jnp.float32),
+            pltpu.SemaphoreType.DMA((2 * count,)),
+        ],
+        compiler_params=pltpu.CompilerParams(vmem_limit_bytes=40 * 2**20),
+        input_output_aliases={0: 0},
+    )(total, *others, *bases)
 
 
 def after(value, *others):
@@ -411,13 +454,15 @@
     total = total + jnp.concatenate(
         [own[kind, chunk] for kind in (0, 1) for chunk in (0, 1)], 1
     )
-    for chunk in (0, 1):
-        total = add_at(
-            total,
-            [after(others[kind, chunk], total) for kind in (0, 1)],
-            [start_of(kind, chunk) for kind in (0, 1)],
-        )
-    return total
+    total = add_at(
+        total,
+        [after(others[kind, 0], total) for kind in (0, 1)],
+        [start_of(kind, 0) for kind in (0, 1)],
+    )
+    starts = [start_of(kind, 1) for kind in (0, 1)]
+    bases = [total[:, start : start + width] for start in starts]
+    last = [after(others[kind, 1], *bases) for kind in (0, 1)]
+    return add_last(total, bases, last, starts)
 
 
 def solution(mesh):

time: 159 us -> 158 us (level)
    pallas_call x2 -> x1, Pallas kernels: 4.91 us -> 2.46 us  [add_at(): pl.pallas_call(functools.partial(add_kernel, starts), in_specs=[anywhere]...]
  transfers between devices with their start and end apart: 17 -> 17, of which waited for: 7 -> 7; matrix products, arithmetic and copies ran while one was open for 4% -> 5% of each run, Pallas kernels for 26% -> 26%
where the time goes in v4:
time: 158 us
  waiting for transfers between devices  86.4 us (55%)
  Pallas kernels  42.6 us (27%)
  starting transfers between devices  20.3 us (13%)
  local copies, waits for them, and re-layouts  4.72 us (3%)
  other arithmetic  3.46 us (2%)
    ppermute x4, waiting for transfers between devices, over_beta(): lax.ppermute(value, 'beta', [(i, i ^ flip) for i in range(beta_devices)])  47.5 us
    ppermute x13, waiting for transfers between devices, over_alpha(): lax.ppermute(value, 'alpha', [(i, i ^ flip) for i in range(alpha_devices)])  38.9 us
    ppermute x13, starting transfers between devices, over_alpha(): lax.ppermute(value, 'alpha', [(i, i ^ flip) for i in range(alpha_devices)])  15.2 us
    pallas_call x4, Pallas kernels, alpha_products(): pl.pallas_call(functools.partial(alpha_kernel, count), grid=(width // til...  14.5 us
    pallas_call x1, Pallas kernels, beta_term(): pl.pallas_call(functools.partial(beta_kernel, layout), in_specs=[smem] *...  12.8 us
    pallas_call x3, Pallas kernels, take(): pl.pallas_call(functools.partial(take_kernel, tuple(places), len(sources)...  7.63 us
    ppermute x4, starting transfers between devices, over_beta(): lax.ppermute(value, 'beta', [(i, i ^ flip) for i in range(beta_devices)])  5.14 us
    pallas_call x1, Pallas kernels, coupling_matrices(): pl.pallas_call(matrix_kernel, in_specs=[pl.BlockSpec(memory_space=pltpu.S...  3.83 us
  transfers between devices with their start and end apart: 17, of which 7 were waited for; matrix products, arithmetic and copies ran while one was open for 5% of the time, Pallas kernels for 26%

profile of v4, /device:TPU:0, one launch (start us, length us, event | category | flops | bytes accessed | tf_op | source)
XLA Modules:
  0.0 157.7 jit_solution(817954849188177303)
XLA Ops:
  0.0 0.5 collective-permute-start
  0.5 2.6 %shard_map.83 = (f32[128,1536]{1,0:T(8,128)}, f32[128,1536]{1,0:T(8,128)}) custom-call(f32[128,6144]{1,0:T(8,128)} %refs_0_.12), custom_call_target="tpu_custom_call" | custom-call | bytes 3145728 | tf_op jit(solution)/shard_map/pallas_call | solution.py:152
  3.1 2.5 %collective-permute-start.3 = (f32[128,1536]{1,0:T(8,128)}, f32[128,1536]{1,0:T(8,128)}, u32[]{:S(2)}, u32[]{:S(2)}) collective-permute-start(f32[128,1536]{1,0:T(8,128)} %get-tuple-element.37), channel_id=1, source_target_pairs={{0,8},{4,12},{8,0},{12,4},{16,24},{20,28},{24,16},{28,20},{1,9},{5... | collective-permute-start | bytes 2359304 | tf_op jit(solution)/shard_map/ppermute | solution.py:362
  5.7 2.6 %collective-permute-start.5 = (f32[128,1536]{1,0:T(8,128)}, f32[128,1536]{1,0:T(8,128)}, u32[]{:S(2)}, u32[]{:S(2)}) collective-permute-start(f32[128,1536]{1,0:T(8,128)} %get-tuple-element.43), channel_id=1, source_target_pairs={{0,16},{4,20},{8,24},{12,28},{16,0},{20,4},{24,8},{28,12},{1,17},{... | collective-permute-start | bytes 2359304 | tf_op jit(solution)/shard_map/ppermute | solution.py:362
  8.3 0.0 collective-permute-done.refs_1_
  8.3 1.6 %collective-permute-start.2 = (f32[128,6144]{1,0:T(8,128)S(1)}, f32[128,6144]{1,0:T(8,128)}, u32[]{:S(2)}, u32[]{:S(2)}) collective-permute-start(f32[128,6144]{1,0:T(8,128)S(1)} %copy-done.1), channel_id=1, source_target_pairs={{0,2},{1,3},{2,0},{3,1},{4,6},{5,7},{6,4},{7,5},{8,10},{9,11},{10,... | collective-permute-start | bytes 9437192 | tf_op jit(solution)/shard_map/ppermute | solution.py:365
  9.9 1.5 collective-permute-start.1
  11.4 0.1 add_bitcast_fusion
  11.4 0.1 copy.30
  11.5 0.1 eq.61
  11.6 0.1 copy.28
  11.7 0.1 eq.53
  11.8 0.1 copy.29
  11.8 0.1 reshape.42
  11.9 0.1 eq.57
  12.1 0.1 add_bitcast_fusion.2
  12.2 0.1 compare_select_fusion
  12.2 0.1 compare_convert_fusion
  12.3 0.2 select_reduce_fusion
  12.5 0.1 reshape.43.weight_ref
  12.6 0.8 fusion
  13.4 0.1 copy.24
  13.5 0.1 rem.16
  13.6 0.1 constant_dynamic-slice_fusion
  13.7 0.1 copy.26
  13.8 0.1 reshape.40.coef_ref
  14.0 0.1 copy.23
  14.1 0.1 div.21.slot_ref
  14.2 0.1 copy.25
  14.3 0.1 reshape.39.kind_ref
  14.5 1.4 pad_bitcast_fusion.1
  15.9 0.1 pad_maximum_fusion
  16.0 0.1 copy.27
  16.1 3.8 %shard_map.82 = (bf16[2,256,512]{2,1,0:T(8,128)(2,1)S(1)}, bf16[2,256,512]{2,1,0:T(8,128)(2,1)S(1)}) custom-call(f32[1024]{0:T(1024)S(1)} %reshape.43.weight_ref, f32[32,64,128]{2,1,0:T(8,128)S(1)} %bitcast.16), custom_call_target="tpu_custom_call" | custom-call | flops 8388608 | bytes 1048576 | tf_op jit(solution)/shard_map/pallas_call | solution.py:70
  20.0 2.7 %shard_map.84 = (f32[128,1536]{1,0:T(8,128)S(1)}, f32[128,1536]{1,0:T(8,128)S(1)}) custom-call(f32[128,6144]{1,0:T(8,128)S(1)} %copy-done.1), custom_call_target="tpu_custom_call" | custom-call | bytes 3145728 | tf_op jit(solution)/shard_map/pallas_call | solution.py:152
  22.7 18.3 %collective-permute-done.3.refs_2_ = f32[128,1536]{1,0:T(8,128)} collective-permute-done((f32[128,1536]{1,0:T(8,128)}, f32[128,1536]{1,0:T(8,128)}, u32[]{:S(2)}, u32[]{:S(2)}) %collective-permute-start.3) | collective-permute-done | bytes 786464 | tf_op jit(solution)/shard_map/ppermute | solution.py:362
  41.0 0.0 collective-permute-start.4
  41.0 2.5 %collective-permute-done.5.refs_2_ = f32[128,1536]{1,0:T(8,128)} collective-permute-done((f32[128,1536]{1,0:T(8,128)}, f32[128,1536]{1,0:T(8,128)}, u32[]{:S(2)}, u32[]{:S(2)}) %collective-permute-start.5) | collective-permute-done | bytes 786464 | tf_op jit(solution)/shard_map/ppermute | solution.py:362
  43.5 0.0 collective-permute-start.6
  43.5 0.3 collective-permute-start.11
  43.9 0.0 collective-permute-done.4.refs_3_
  43.9 2.7 %collective-permute-start.9 = (f32[128,1536]{1,0:T(8,128)S(1)}, f32[128,1536]{1,0:T(8,128)S(1)}, u32[]{:S(2)}, u32[]{:S(2)}) collective-permute-start(f32[128,1536]{1,0:T(8,128)S(1)} %get-tuple-element.40), channel_id=1, source_target_pairs={{0,8},{4,12},{8,0},{12,4},{16,24},{20,28},{24,16},{28,20},{1,9},{5... | collective-permute-start | bytes 2359304 | tf_op jit(solution)/shard_map/ppermute | solution.py:362
  46.6 3.3 %shard_map.85 = (f32[128,1536]{1,0:T(8,128)S(1)}, f32[128,1536]{1,0:T(8,128)S(1)}) custom-call(bf16[2,256,512]{2,1,0:T(8,128)(2,1)S(1)} %get-tuple-element.35.high_ref, bf16[2,256,512]{2,1,0:T(8,128)(2,1)S(1)} %get-tuple-element.36.low_ref, f32[128,6144]{1,0:T(8,128)S(1)} %copy-done.1, f32[128,6144]{1,0:T(8,128)} %collective-permute-done.refs_1_, ...), custom_call_target="tpu_custom_call" | custom-call | flops 1207959552 | bytes 4718592 | tf_op jit(solution)/shard_map/pallas_call | solution.py:103
  49.9 4.1 %shard_map.86 = (f32[128,1536]{1,0:T(8,128)S(1)}, f32[128,1536]{1,0:T(8,128)}) custom-call(bf16[2,256,512]{2,1,0:T(8,128)(2,1)S(1)} %get-tuple-element.35.high_ref, bf16[2,256,512]{2,1,0:T(8,128)(2,1)S(1)} %get-tuple-element.36.low_ref, f32[128,6144]{1,0:T(8,128)S(1)} %copy-done.1, f32[128,6144]{1,0:T(8,128)} %collective-permute-done.refs_1_, ...), custom_call_target="tpu_custom_call" | custom-call | flops 1207959552 | bytes 4718592 | tf_op jit(solution)/shard_map/pallas_call | solution.py:103
  54.0 24.5 %collective-permute-done.2.refs_0_.refs_2_ = f32[128,6144]{1,0:T(8,128)} collective-permute-done((f32[128,6144]{1,0:T(8,128)S(1)}, f32[128,6144]{1,0:T(8,128)}, u32[]{:S(2)}, u32[]{:S(2)}) %collective-permute-start.2) | collective-permute-done | bytes 3145760 | tf_op jit(solution)/shard_map/ppermute | solution.py:365
  78.5 1.2 collective-permute-done.1.refs_1_
  79.7 2.4 %shard_map.87 = (f32[64,6144]{1,0:T(8,128)}, f32[64,6144]{1,0:T(8,128)S(1)}) custom-call(f32[128,6144]{1,0:T(8,128)} %collective-permute-done.2.refs_0_.refs_2_, f32[128,6144]{1,0:T(8,128)} %collective-permute-done.1.refs_1_), custom_call_target="tpu_custom_call" | custom-call | bytes 6291456 | tf_op jit(solution)/shard_map/pallas_call | solution.py:152
  82.1 1.6 collective-permute-start.7
  83.6 0.5 collective-permute-start.8
  84.2 0.5 collective-permute-start.10
  84.7 1.9 %collective-permute-start.13 = (f32[128,1536]{1,0:T(8,128)S(1)}, f32[128,1536]{1,0:T(8,128)S(1)}, u32[]{:S(2)}, u32[]{:S(2)}) collective-permute-start(f32[128,1536]{1,0:T(8,128)S(1)} %get-tuple-element.42), channel_id=1, source_target_pairs={{0,16},{4,20},{8,24},{12,28},{16,0},{20,4},{24,8},{28,12},{1,17},{... | collective-permute-start | bytes 2359304 | tf_op jit(solution)/shard_map/ppermute | solution.py:362
  86.6 1.6 collective-permute-start.14
  88.2 3.9 %shard_map.90 = (f32[128,1536]{1,0:T(8,128)S(1)}, f32[128,1536]{1,0:T(8,128)}) custom-call(bf16[2,256,512]{2,1,0:T(8,128)(2,1)S(1)} %get-tuple-element.35.high_ref, bf16[2,256,512]{2,1,0:T(8,128)(2,1)S(1)} %get-tuple-element.36.low_ref, f32[128,6144]{1,0:T(8,128)S(1)} %copy-done.1, f32[128,6144]{1,0:T(8,128)} %collective-permute-done.refs_1_, ...), custom_call_target="tpu_custom_call" | custom-call | flops 1207959552 | bytes 4718592 | tf_op jit(solution)/shard_map/pallas_call | solution.py:103
  92.1 0.4 collective-permute-start.16
  92.5 3.2 %shard_map.89 = (f32[128,1536]{1,0:T(8,128)S(1)}, f32[128,1536]{1,0:T(8,128)S(1)}) custom-call(bf16[2,256,512]{2,1,0:T(8,128)(2,1)S(1)} %get-tuple-element.35.high_ref, bf16[2,256,512]{2,1,0:T(8,128)(2,1)S(1)} %get-tuple-element.36.low_ref, f32[128,6144]{1,0:T(8,128)S(1)} %copy-done.1, f32[128,6144]{1,0:T(8,128)} %collective-permute-done.refs_1_, ...), custom_call_target="tpu_custom_call" | custom-call | flops 1207959552 | bytes 4718592 | tf_op jit(solution)/shard_map/pallas_call | solution.py:103
  95.7 21.8 %collective-permute-done.7.refs_3_ = f32[64,6144]{1,0:T(8,128)S(1)} collective-permute-done((f32[64,6144]{1,0:T(8,128)}, f32[64,6144]{1,0:T(8,128)S(1)}, u32[]{:S(2)}, u32[]{:S(2)}) %collective-permute-start.7) | collective-permute-done | bytes 1572896 | tf_op jit(solution)/shard_map/ppermute | solution.py:365
  117.5 2.0 %collective-permute-start.15 = (f32[128,1536]{1,0:T(8,128)S(1)}, f32[128,1536]{1,0:T(8,128)S(1)}, u32[]{:S(2)}, u32[]{:S(2)}) collective-permute-start(f32[128,1536]{1,0:T(8,128)S(1)} %get-tuple-element.57), channel_id=1, source_target_pairs={{0,16},{4,20},{8,24},{12,28},{16,0},{20,4},{24,8},{28,12},{1,17},{... | collective-permute-start | bytes 2359304 | tf_op jit(solution)/shard_map/ppermute | solution.py:362
  119.6 12.8 %shard_map.88 = f32[128,6144]{1,0:T(8,128)S(1)} custom-call(s32[1]{0:T(128)} %bitcast.me_ref, s32[192]{0:T(256)S(1)} %div.21.slot_ref, s32[192]{0:T(256)S(1)} %get-tuple-element.70.tile_ref, s32[192]{0:T(256)S(1)} %get-tuple-element.69.half_ref, s32[192]{0:T(256)S(1)} %reshape.39.kind_ref, f32[192]{0:T(256)S(1)} %reshape.40.coef_ref, ...), custom_call_target="tpu_custom_call" | custom-call | flops 2415919104 | bytes 15728640 | tf_op jit(solution)/shard_map/pallas_call | solution.py:324
  132.3 2.0 %maximum_add_fusion.total_ref = f32[128,6144]{1,0:T(8,128)} fusion(f32[128,6144]{1,0:T(8,128)S(1)} %shard_map.88, f32[128,1536]{1,0:T(8,128)S(1)} %get-tuple-element.54, f32[128,1536]{1,0:T(8,128)S(1)} %get-tuple-element.52, f32[128,1536]{1,0:T(8,128)S(1)} %get-tuple-element.51, f32[128,1536]{1,0:T(8,128)S(1)} %get-tuple-element.49), kind=kLoop, calls=%fused_computation | loop fusion | flops 3145728 | bytes 9437184 | tf_op jit(solution)/shard_map/add | solution.py:454
  134.4 6.1 %collective-permute-done.14.refs_1_ = f32[128,1536]{1,0:T(8,128)S(1)} collective-permute-done((f32[128,1536]{1,0:T(8,128)}, f32[128,1536]{1,0:T(8,128)S(1)}, u32[]{:S(2)}, u32[]{:S(2)}) %collective-permute-start.14) | collective-permute-done | bytes 786464 | tf_op jit(solution)/shard_map/ppermute | solution.py:362
  140.5 2.5 %shard_map.91.refs_0_ = f32[128,6144]{1,0:T(8,128)} custom-call(f32[128,6144]{1,0:T(8,128)} %maximum_add_fusion.total_ref, f32[128,1536]{1,0:T(8,128)S(1)} %collective-permute-done.13.refs_0_, f32[128,1536]{1,0:T(8,128)S(1)} %collective-permute-done.14.refs_1_), custom_call_target="tpu_custom_call", output_to_operand_aliasing={{}: (0, {})} | custom-call | tf_op jit(solution)/shard_map/pallas_call | solution.py:204
  142.9 1.5 fusion.2
  144.4 11.9 %collective-permute-done.16.refs_2_ = f32[128,1536]{1,0:T(8,128)S(1)} collective-permute-done((f32[128,1536]{1,0:T(8,128)}, f32[128,1536]{1,0:T(8,128)S(1)}, u32[]{:S(2)}, u32[]{:S(2)}) %collective-permute-start.16) | collective-permute-done | bytes 786464 | tf_op jit(solution)/shard_map/ppermute | solution.py:362
  156.4 1.4 shard_map.92
  (28 shorter events, 0.1 us)
Async XLA Ops:
  0.0 13.6 %copy-start = (f32[384,2]{0,1:T(2,128)S(1)}, f32[384,2]{0,1:T(2,128)}, u32[]{:S(2)}) copy-start(f32[384,2]{0,1:T(2,128)} %param.15) | copy-start | bytes 9220
  0.0 8.3 %copy-start.1 = (f32[128,6144]{1,0:T(8,128)S(1)}, f32[128,6144]{1,0:T(8,128)}, u32[]{:S(2)}) copy-start(f32[128,6144]{1,0:T(8,128)} %refs_0_.12) | copy-start | bytes 9437188
  0.0 11.4 %copy-start.2 = (s32[16,8]{0,1:T(8,128)S(1)}, s32[16,8]{0,1:T(8,128)}, u32[]{:S(2)}) copy-start(s32[16,8]{0,1:T(8,128)} %param.10) | copy-start | bytes 1540
  0.0 11.6 %copy-start.3 = (s32[16,8]{0,1:T(8,128)S(1)}, s32[16,8]{0,1:T(8,128)}, u32[]{:S(2)}) copy-start(s32[16,8]{0,1:T(8,128)} %param.11) | copy-start | bytes 1540
  0.0 11.8 %copy-start.4 = (f32[16,8]{0,1:T(8,128)S(1)}, f32[16,8]{0,1:T(8,128)}, u32[]{:S(2)}) copy-start(f32[16,8]{0,1:T(8,128)} %param.12) | copy-start | bytes 1540
  0.0 8.2 %collective-permute-start = (f32[128,6144]{1,0:T(8,128)}, f32[128,6144]{1,0:T(8,128)}, u32[]{:S(2)}, u32[]{:S(2)}) collective-permute-start(f32[128,6144]{1,0:T(8,128)} %refs_0_.12), channel_id=1, source_target_pairs={{0,4},{4,0},{8,12},{12,8},{16,20},{20,16},{24,28},{28,24},{1,5},{5... | collective-permute-start | bytes 9437192 | tf_op jit(solution)/shard_map/ppermute | solution.py:362
  3.1 37.9 %collective-permute-start.3 = (f32[128,1536]{1,0:T(8,128)}, f32[128,1536]{1,0:T(8,128)}, u32[]{:S(2)}, u32[]{:S(2)}) collective-permute-start(f32[128,1536]{1,0:T(8,128)} %get-tuple-element.37), channel_id=1, source_target_pairs={{0,8},{4,12},{8,0},{12,4},{16,24},{20,28},{24,16},{28,20},{1,9},{5... | collective-permute-start | bytes 2359304 | tf_op jit(solution)/shard_map/ppermute | solution.py:362
  5.7 37.9 %collective-permute-start.5 = (f32[128,1536]{1,0:T(8,128)}, f32[128,1536]{1,0:T(8,128)}, u32[]{:S(2)}, u32[]{:S(2)}) collective-permute-start(f32[128,1536]{1,0:T(8,128)} %get-tuple-element.43), channel_id=1, source_target_pairs={{0,16},{4,20},{8,24},{12,28},{16,0},{20,4},{24,8},{28,12},{1,17},{... | collective-permute-start | bytes 2359304 | tf_op jit(solution)/shard_map/ppermute | solution.py:362
  8.3 70.2 %collective-permute-start.2 = (f32[128,6144]{1,0:T(8,128)S(1)}, f32[128,6144]{1,0:T(8,128)}, u32[]{:S(2)}, u32[]{:S(2)}) collective-permute-start(f32[128,6144]{1,0:T(8,128)S(1)} %copy-done.1), channel_id=1, source_target_pairs={{0,2},{1,3},{2,0},{3,1},{4,6},{5,7},{6,4},{7,5},{8,10},{9,11},{10,... | collective-permute-start | bytes 9437192 | tf_op jit(solution)/shard_map/ppermute | solution.py:365
  9.9 69.9 %collective-permute-start.1 = (f32[128,6144]{1,0:T(8,128)S(1)}, f32[128,6144]{1,0:T(8,128)}, u32[]{:S(2)}, u32[]{:S(2)}) collective-permute-start(f32[128,6144]{1,0:T(8,128)S(1)} %copy-done.1), channel_id=1, source_target_pairs={{0,1},{1,0},{2,3},{3,2},{4,5},{5,4},{6,7},{7,6},{8,9},{9,8},{10,11... | collective-permute-start | bytes 9437192 | tf_op jit(solution)/shard_map/ppermute | solution.py:365
  41.0 2.9 %collective-permute-start.4 = (f32[128,1536]{1,0:T(8,128)}, f32[128,1536]{1,0:T(8,128)S(1)}, u32[]{:S(2)}, u32[]{:S(2)}) collective-permute-start(f32[128,1536]{1,0:T(8,128)} %collective-permute-done.3.refs_2_), channel_id=1, source_target_pairs={{0,4},{4,0},{8,12},{12,8},{16,20},{20,16},{24,28},{28,24},{1,5},{5... | collective-permute-start | bytes 2359304 | tf_op jit(solution)/shard_map/ppermute | solution.py:362
  43.5 6.4 %collective-permute-start.6 = (f32[128,1536]{1,0:T(8,128)}, f32[128,1536]{1,0:T(8,128)S(1)}, u32[]{:S(2)}, u32[]{:S(2)}) collective-permute-start(f32[128,1536]{1,0:T(8,128)} %collective-permute-done.5.refs_2_), channel_id=1, source_target_pairs={{0,4},{4,0},{8,12},{12,8},{16,20},{20,16},{24,28},{28,24},{1,5},{5... | collective-permute-start | bytes 2359304 | tf_op jit(solution)/shard_map/ppermute | solution.py:362
  43.5 40.6 %collective-permute-start.11 = (f32[128,1536]{1,0:T(8,128)S(1)}, f32[128,1536]{1,0:T(8,128)S(1)}, u32[]{:S(2)}, u32[]{:S(2)}) collective-permute-start(f32[128,1536]{1,0:T(8,128)S(1)} %get-tuple-element.39), channel_id=1, source_target_pairs={{0,16},{4,20},{8,24},{12,28},{16,0},{20,4},{24,8},{28,12},{1,17},{... | collective-permute-start | bytes 2359304 | tf_op jit(solution)/shard_map/ppermute | solution.py:362
  43.9 40.3 %collective-permute-start.9 = (f32[128,1536]{1,0:T(8,128)S(1)}, f32[128,1536]{1,0:T(8,128)S(1)}, u32[]{:S(2)}, u32[]{:S(2)}) collective-permute-start(f32[128,1536]{1,0:T(8,128)S(1)} %get-tuple-element.40), channel_id=1, source_target_pairs={{0,8},{4,12},{8,0},{12,4},{16,24},{20,28},{24,16},{28,20},{1,9},{5... | collective-permute-start | bytes 2359304 | tf_op jit(solution)/shard_map/ppermute | solution.py:362
  82.1 35.4 %collective-permute-start.7 = (f32[64,6144]{1,0:T(8,128)}, f32[64,6144]{1,0:T(8,128)S(1)}, u32[]{:S(2)}, u32[]{:S(2)}) collective-permute-start(f32[64,6144]{1,0:T(8,128)} %get-tuple-element.47), channel_id=1, source_target_pairs={{0,1},{1,0},{2,3},{3,2},{4,5},{5,4},{6,7},{7,6},{8,9},{9,8},{10,11... | collective-permute-start | bytes 4718600 | tf_op jit(solution)/shard_map/ppermute | solution.py:365
  83.6 35.9 %collective-permute-start.8 = (f32[64,6144]{1,0:T(8,128)S(1)}, f32[64,6144]{1,0:T(8,128)S(1)}, u32[]{:S(2)}, u32[]{:S(2)}) collective-permute-start(f32[64,6144]{1,0:T(8,128)S(1)} %get-tuple-element.48), channel_id=1, source_target_pairs={{0,2},{1,3},{2,0},{3,1},{4,6},{5,7},{6,4},{7,5},{8,10},{9,11},{10,... | collective-permute-start | bytes 4718600 | tf_op jit(solution)/shard_map/ppermute | solution.py:365
  84.2 2.4 %collective-permute-start.12 = (f32[128,1536]{1,0:T(8,128)S(1)}, f32[128,1536]{1,0:T(8,128)S(1)}, u32[]{:S(2)}, u32[]{:S(2)}) collective-permute-start(f32[128,1536]{1,0:T(8,128)S(1)} %collective-permute-done.11.refs_2_), channel_id=1, source_target_pairs={{0,4},{4,0},{8,12},{12,8},{16,20},{20,16},{24,28},{28,24},{1,5},{5... | collective-permute-start | bytes 2359304 | tf_op jit(solution)/shard_map/ppermute | solution.py:362
  84.2 7.9 %collective-permute-start.10 = (f32[128,1536]{1,0:T(8,128)S(1)}, f32[128,1536]{1,0:T(8,128)S(1)}, u32[]{:S(2)}, u32[]{:S(2)}) collective-permute-start(f32[128,1536]{1,0:T(8,128)S(1)} %collective-permute-done.9.refs_2_), channel_id=1, source_target_pairs={{0,4},{4,0},{8,12},{12,8},{16,20},{20,16},{24,28},{28,24},{1,5},{5... | collective-permute-start | bytes 2359304 | tf_op jit(solution)/shard_map/ppermute | solution.py:362
  84.7 55.8 %collective-permute-start.13 = (f32[128,1536]{1,0:T(8,128)S(1)}, f32[128,1536]{1,0:T(8,128)S(1)}, u32[]{:S(2)}, u32[]{:S(2)}) collective-permute-start(f32[128,1536]{1,0:T(8,128)S(1)} %get-tuple-element.42), channel_id=1, source_target_pairs={{0,16},{4,20},{8,24},{12,28},{16,0},{20,4},{24,8},{28,12},{1,17},{... | collective-permute-start | bytes 2359304 | tf_op jit(solution)/shard_map/ppermute | solution.py:362
  86.6 53.9 %collective-permute-start.14 = (f32[128,1536]{1,0:T(8,128)}, f32[128,1536]{1,0:T(8,128)S(1)}, u32[]{:S(2)}, u32[]{:S(2)}) collective-permute-start(f32[128,1536]{1,0:T(8,128)} %get-tuple-element.45), channel_id=1, source_target_pairs={{0,8},{4,12},{8,0},{12,4},{16,24},{20,28},{24,16},{28,20},{1,9},{5... | collective-permute-start | bytes 2359304 | tf_op jit(solution)/shard_map/ppermute | solution.py:362
  92.1 64.3 %collective-permute-start.16 = (f32[128,1536]{1,0:T(8,128)}, f32[128,1536]{1,0:T(8,128)S(1)}, u32[]{:S(2)}, u32[]{:S(2)}) collective-permute-start(f32[128,1536]{1,0:T(8,128)} %get-tuple-element.59), channel_id=1, source_target_pairs={{0,8},{4,12},{8,0},{12,4},{16,24},{20,28},{24,16},{28,20},{1,9},{5... | collective-permute-start | bytes 2359304 | tf_op jit(solution)/shard_map/ppermute | solution.py:362
  117.5 38.8 %collective-permute-start.15 = (f32[128,1536]{1,0:T(8,128)S(1)}, f32[128,1536]{1,0:T(8,128)S(1)}, u32[]{:S(2)}, u32[]{:S(2)}) collective-permute-start(f32[128,1536]{1,0:T(8,128)S(1)} %get-tuple-element.57), channel_id=1, source_target_pairs={{0,16},{4,20},{8,24},{12,28},{16,0},{20,4},{24,8},{28,12},{1,17},{... | collective-permute-start | bytes 2359304 | tf_op jit(solution)/shard_map/ppermute | solution.py:362
